TPU v7x, 32 devices: a whole 2x2x4 slice. The times are simulated.
32 devices in a mesh: row: 4 (over z), col: 8 (over y, x, core).
Axes of the slice: x: 2, y: 2, z: 4, core: 2. Of those that a mesh axis runs over, the one named last changes fastest.
Arguments:
- features: bfloat16 [65536, 256], P(('row', 'col')), may hold values from -6 to 6
- cotangent: bfloat16 [65536, 256], P(('row', 'col')), may hold values from -6 to 6
- tile_values: bfloat16 [512, 4, 4, 128, 128], P(('row', 'col')), may hold values from -0.25 to 0.25
- tile_src: int32 [512, 4, 4], P(('row', 'col')), may hold values from 0 to 17
- tile_count: int32 [512, 4], P(('row', 'col')), may hold values from 1 to 4
- send_rows: int32 [32, 32, 8], P(('row', 'col')), may hold values from 0 to 2047
- w_stack: bfloat16 [1280, 256], replicated, may hold values from -0.375 to 0.375
- w_qkv: bfloat16 [256, 768], replicated, may hold values from -0.375 to 0.375
Outputs:
- layer_out: bfloat16 [65536, 256], P(('row', 'col'))
- input_grad: bfloat16 [65536, 256], P(('row', 'col'))
- stack_grad: float32 [1280, 256], replicated
- qkv_grad: float32 [256, 768], replicated
Inputs may be any that keep to these rules, and one draw needn't show every extreme that they name: `tile_src`: a tile of the partition's own rows (below 16) or of its received boundary rows. `send_rows`: a row of the sending partition.
All inputs are finite; a program needn't handle non-finite values.
Results may differ from a plain program's by a relative error of at most 0.0061.
Values may be sent and summed in bfloat16 or wider, within the bound.
A program may use at most 128 MiB of HBM per device.

v0:
```python
import jax
import jax.numpy as jnp
from jax import lax
from jax.sharding import PartitionSpec as P

HEADS = 4
RELS = 4
TILE = 128


def local(features, cotangent, tile_values, tile_src, tile_count, send_rows, w_stack, w_qkv):
    node_dev, width = features.shape
    row_count = lax.axis_size("row")
    col_count = lax.axis_size("col")
    devices = row_count * col_count
    tiles = node_dev // TILE
    bound = send_rows.shape[2]
    span = tiles + devices * bound // TILE
    head_dim = width // HEADS
    node_scale = 1.0 / jnp.sqrt(jnp.float32(node_dev * devices))
    head_scale = 1.0 / jnp.sqrt(jnp.float32(head_dim))
    highest = lax.Precision.HIGHEST
    my_rows = send_rows[0]
    outgoing = features[my_rows]
    incoming = lax.all_to_all(outgoing, ("row", "col"), split_axis=0, concat_axis=0, tiled=True)
    extended = jnp.concatenate(
        [features, incoming.reshape(devices * bound, width)], axis=0
    ).reshape(span, TILE, width)
    slots = lax.broadcasted_iota(jnp.int32, tile_src.shape, 2)
    active = slots < tile_count[:, :, None]
    masked = jnp.where(active[..., None, None], tile_values, jnp.zeros((), tile_values.dtype))
    relation_msgs = []
    for relation in range(RELS):
        picked = extended[tile_src[:, relation]]
        message = jnp.einsum(
            "tsij,tsjh->tih", masked[:, relation], picked, preferred_element_type=jnp.float32
        )
        relation_msgs.append(message.reshape(node_dev, width).astype(jnp.bfloat16))
    joined = jnp.concatenate([features] + relation_msgs, axis=1)
    pre = jnp.dot(joined, w_stack, preferred_element_type=jnp.float32)
    qkv = jnp.dot(features, w_qkv, preferred_element_type=jnp.float32).astype(jnp.bfloat16)
    query = qkv[:, :width].reshape(node_dev, HEADS, head_dim)
    keys = qkv[:, width : 2 * width].reshape(node_dev, HEADS, head_dim)
    vals = qkv[:, 2 * width :].reshape(node_dev, HEADS, head_dim)
    local_state = (
        jnp.einsum("nha,nhb->hab", keys, vals, preferred_element_type=jnp.float32) * node_scale
    )
    kv_state = lax.psum(local_state, ("row", "col"))
    attended = (
        jnp.einsum("nha,hab->nhb", query.astype(jnp.float32), kv_state, precision=highest)
        * head_scale
    )
    activated, pull_back = jax.vjp(jax.nn.gelu, pre)
    layer_out = (activated + attended.reshape(node_dev, width)).astype(jnp.bfloat16)
    grad_out = cotangent.astype(jnp.float32)
    grad_pre = pull_back(grad_out)[0].astype(jnp.bfloat16)
    grad_back = lax.dot_general(
        grad_pre, w_stack, (((1,), (1,)), ((), ())), preferred_element_type=jnp.float32
    )
    stack_part = lax.dot_general(
        joined, grad_pre, (((0,), (0,)), ((), ())), preferred_element_type=jnp.float32
    )
    ext_grad = jnp.zeros((span, TILE, width), jnp.float32)
    for relation in range(RELS):
        pulled = (
            grad_back[:, (relation + 1) * width : (relation + 2) * width]
            .astype(jnp.bfloat16)
            .reshape(tiles, TILE, width)
        )
        spread = jnp.einsum(
            "tsij,tih->tsjh", masked[:, relation], pulled, preferred_element_type=jnp.float32
        )
        ext_grad = ext_grad.at[tile_src[:, relation].reshape(-1)].add(
            spread.reshape(-1, TILE, width)
        )
    halo_grad = ext_grad[tiles:].reshape(devices, bound, width).astype(jnp.bfloat16)
    returned = lax.all_to_all(halo_grad, ("row", "col"), split_axis=0, concat_axis=0, tiled=True)
    scattered = (
        jnp.zeros((node_dev, width), jnp.float32)
        .at[my_rows.reshape(devices * bound)]
        .add(returned.reshape(devices * bound, width).astype(jnp.float32))
    )
    gcn_grad = grad_back[:, :width] + ext_grad[:tiles].reshape(node_dev, width) + scattered
    grad_heads = cotangent.reshape(node_dev, HEADS, head_dim)
    partial_state = (
        jnp.einsum("nha,nhb->hab", query, grad_heads, preferred_element_type=jnp.float32)
        * head_scale
    )
    grad_query = (
        jnp.einsum(
            "nhb,hab->nha", grad_out.reshape(node_dev, HEADS, head_dim), kv_state, precision=highest
        )
        * head_scale
    )
    grad_query = grad_query.reshape(node_dev, width)
    features_wide = features.astype(jnp.float32)
    query_part = lax.dot_general(
        features_wide, grad_query, (((0,), (0,)), ((), ())), precision=highest
    )
    key_moment = lax.dot_general(
        features,
        qkv[:, width : 2 * width],
        (((0,), (0,)), ((), ())),
        preferred_element_type=jnp.float32,
    )
    value_moment = lax.dot_general(
        features, qkv[:, 2 * width :], (((0,), (0,)), ((), ())), preferred_element_type=jnp.float32
    )
    state_grad, stack_grad, query_grad, key_total, value_total = lax.psum(
        (partial_state, stack_part, query_part, key_moment, value_moment), ("row", "col")
    )
    key_weight = (
        jnp.einsum(
            "ihb,hab->iha",
            value_total.reshape(width, HEADS, head_dim),
            state_grad,
            precision=highest,
        )
        * node_scale
    )
    value_weight = (
        jnp.einsum(
            "iha,hab->ihb", key_total.reshape(width, HEADS, head_dim), state_grad, precision=highest
        )
        * node_scale
    )
    qkv_grad = jnp.concatenate(
        [query_grad, key_weight.reshape(width, width), value_weight.reshape(width, width)], axis=1
    )
    grad_keys = (
        jnp.einsum("nhb,hab->nha", vals.astype(jnp.float32), state_grad, precision=highest)
        * node_scale
    )
    grad_vals = (
        jnp.einsum("nha,hab->nhb", keys.astype(jnp.float32), state_grad, precision=highest)
        * node_scale
    )
    dqkv = jnp.concatenate(
        [grad_query, grad_keys.reshape(node_dev, width), grad_vals.reshape(node_dev, width)], axis=1
    )
    dqkv_low = dqkv.astype(jnp.bfloat16)
    attn_back = lax.dot_general(
        dqkv_low, w_qkv, (((1,), (1,)), ((), ())), preferred_element_type=jnp.float32
    )
    input_grad = (gcn_grad + attn_back).astype(jnp.bfloat16)
    return (layer_out, input_grad, stack_grad, qkv_grad)


def solution(mesh):
    placed = (
        P(("row", "col"), None),
        P(("row", "col"), None),
        P(("row", "col"), None, None, None, None),
        P(("row", "col"), None, None),
        P(("row", "col"), None),
        P(("row", "col"), None, None),
        P(),
        P(),
    )
    return jax.shard_map(
        local,
        mesh=mesh,
        in_specs=placed,
        out_specs=(P(("row", "col"), None), P(("row", "col"), None), P(), P()),
        check_vma=False,
    )
```

profile of v0, /device:TPU:0, one launch (start us, length us, event | category | flops | bytes accessed | tf_op | source)
XLA Modules:
  0.0 360.6 jit_solution(4969940647717492393)
XLA Ops:
  7.2 2.4 convolution_convert_fusion
  9.6 1.6 fusion.46
  12.9 1.1 convolution_multiply_fusion.7
  14.2 1.8 gather_fusion
  16.0 7.3 %all-to-all-start = ((bf16[32,8,256]{2,1,0:T(8,128)(2,1)}), bf16[32,8,256]{2,1,0:T(8,128)(2,1)S(1)}, u32[]{:S(2)}, u32[]{:S(2)}) async-start(bf16[32,8,256]{2,1,0:T(8,128)(2,1)} %bitcast.2), calls=%async_computation | async-start | bytes 262144 | tf_op jit(solution)/shard_map/all_to_all | solution.py:25
  23.4 1.2 constant_dynamic-update-slice_fusion.4
  24.6 2.4 fusion.39
  27.0 2.4 fusion.37
  30.2 1.5 copy.48
  32.6 7.3 %copy_select_fusion = bf16[16,4,4,128,128]{4,3,2,0,1:T(8,128)(2,1)} fusion(bf16[16,4,4,128,128]{4,3,2,1,0:T(8,128)(2,1)} %param.10, pred[16,4,4]{2,0,1:T(8,128)(4,1)S(1)} %iota_compare_fusion), kind=kLoop, calls=%fused_computation.10 | loop fusion | flops 4194304 | bytes 16777472 | tf_op jit(solution)/shard_map/jit(_where)/select_n | solution.py:31
  39.9 1.2 convolution_multiply_fusion.6
  41.1 98.4 %all-reduce.4.cloned.1.call-done = f32[4,64,64]{2,1,0:T(8,128)} async-done(((f32[4,64,64]{2,1,0:T(8,128)}), f32[4,64,64]{2,1,0:T(8,128)}) %all-reduce.4.cloned.1.call-update) | async-done | bytes 65552 | tf_op jit(solution)/shard_map/psum | solution.py:48
  139.5 3.6 %convolution_multiply_fusion.3 = f32[4,64,2048]{2,1,0:T(8,128)} fusion(f32[4,64,64]{2,1,0:T(8,128)} %all-reduce.4.cloned.1.call-done, bf16[2048,4,64]{0,2,1:T(8,128)(2,1)} %bitcast.197), kind=kOutput, calls=%fused_computation.23 | convolution fusion | flops 403177472 | bytes 3211264 | tf_op jit(solution)/shard_map/nha,hab->nhb/dot_general | solution.py:50
  143.1 3.0 copy.39
  147.1 1.1 bitcast_convert_fusion.4
  148.2 1.8 convolution_bitcast_fusion
  150.1 2.9 gather_fusion.1
  153.0 2.8 gather_fusion.2
  155.8 3.8 %bitcast_convert_fusion.3 = bf16[16,128,256]{2,1,0:T(8,128)(2,1)S(1)} fusion(bf16[16,4,128,256]{3,2,1,0:T(8,128)(2,1)} %bitcast.191, bf16[16,4,4,128,128]{4,3,2,0,1:T(8,128)(2,1)} %copy_select_fusion), kind=kOutput, calls=%fused_computation.47 | convolution fusion | flops 537395200 | bytes 7340032 | tf_op jit(solution)/shard_map/tsij,tsjh->tih/dot_general | solution.py:35
  159.8 3.4 bitcast_convert_fusion.2
  163.2 2.9 gather_fusion.3
  166.1 4.6 %bitcast_convert_fusion.1 = bf16[16,128,256]{2,1,0:T(8,128)(2,1)} fusion(bf16[16,4,128,256]{3,2,1,0:T(8,128)(2,1)} %bitcast.194, bf16[16,4,4,128,128]{4,3,2,0,1:T(8,128)(2,1)} %copy_select_fusion), kind=kOutput, calls=%fused_computation.45 | convolution fusion | flops 537395200 | bytes 7340032 | tf_op jit(solution)/shard_map/tsij,tsjh->tih/dot_general | solution.py:35
  170.7 2.9 gather_fusion.4
  173.6 3.7 %bitcast_convert_fusion = bf16[16,128,256]{2,1,0:T(8,128)(2,1)S(1)} fusion(bf16[16,4,128,256]{3,2,1,0:T(8,128)(2,1)} %bitcast.193, bf16[16,4,4,128,128]{4,3,2,0,1:T(8,128)(2,1)} %copy_select_fusion), kind=kOutput, calls=%fused_computation.44 | convolution fusion | flops 537395200 | bytes 7340032 | tf_op jit(solution)/shard_map/tsij,tsjh->tih/dot_general | solution.py:35
  177.3 1.2 constant_dynamic-update-slice_fusion.3
  178.9 1.2 constant_dynamic-update-slice_fusion.2
  180.1 1.1 constant_dynamic-update-slice_fusion.1
  181.2 1.1 constant_dynamic-update-slice_fusion
  182.3 5.6 %add_convert_fusion = (bf16[2048,256]{1,0:T(8,128)(2,1)}, f32[2048,256]{1,0:T(8,128)S(1)}) fusion(f32[2048,256]{1,0:T(8,128)S(1)} %copy-done.13, bf16[2048,1280]{1,0:T(8,128)(2,1)} %constant_dynamic-update-slice_fusion, bf16[1280,256]{1,0:T(8,128)(2,1)S(1)} %copy-done), kind=kOutput, calls=%fused_computation.48 | convolution fusion | flops 1347420160 | bytes 11141120 | tf_op jit(solution)/shard_map/dot_general | solution.py:40
  187.9 3.3 fusion.41
  191.2 5.5 %fusion.48 = (bf16[2048,1280]{1,0:T(8,128)(2,1)S(1)}, f32[2048,1280]{1,0:T(8,128)}) fusion(bf16[1280,256]{1,0:T(8,128)(2,1)S(1)} %copy-done, bf16[2048,256]{1,0:T(8,128)(2,1)S(1)} %copy-done.9, f32[2048,256]{1,0:T(8,128)S(1)} %get-tuple-element.33), kind=kOutput, calls=%fused_computation.104 | convolution fusion | flops 1355808768 | bytes 19529728 | tf_op jit(solution)/shard_map/dot_general | solution.py:57
  196.7 1.6 fusion.45
  198.3 6.3 %fusion.21 = f32[16,4,128,256]{3,2,1,0:T(8,128)} fusion(bf16[16,128,256,1]{2,1,3,0:T(8,128)(2,1)S(1)} %bitcast.211, bf16[16,4,4,128,128]{4,3,2,0,1:T(8,128)(2,1)} %copy_select_fusion), kind=kOutput, calls=%fused_computation.49 | convolution fusion | flops 536870912 | bytes 11534336 | tf_op jit(solution)/shard_map/tsij,tih->tsjh/dot_general | solution.py:70
  204.6 6.2 %fusion.23 = f32[16,4,128,256]{3,2,1,0:T(8,128)} fusion(bf16[16,128,256,1]{2,1,3,0:T(8,128)(2,1)S(1)} %bitcast.210, bf16[16,4,4,128,128]{4,3,2,0,1:T(8,128)(2,1)} %copy_select_fusion), kind=kOutput, calls=%fused_computation.51 | convolution fusion | flops 536870912 | bytes 11534336 | tf_op jit(solution)/shard_map/tsij,tih->tsjh/dot_general | solution.py:70
  211.0 12.5 %scatter_fusion = f32[18,128,256]{2,1,0:T(8,128)S(1)} fusion(f32[18,128,256]{2,1,0:T(8,128)S(1)} %broadcast_in_dim.16, s32[64]{0:T(128)S(1)} %fusion.32, f32[64,128,256]{2,1,0:T(8,128)} %bitcast.186), kind=kCustom, calls=%fused_computation.5 | custom fusion | flops 2097152 | bytes 25166080 | tf_op jit(solution)/shard_map/scatter-add | solution.py:73
  223.5 12.5 %scatter_fusion.1 = f32[18,128,256]{2,1,0:T(8,128)S(1)} fusion(f32[18,128,256]{2,1,0:T(8,128)S(1)} %scatter_fusion, s32[64]{0:T(128)S(1)} %fusion.33, f32[64,128,256]{2,1,0:T(8,128)} %bitcast.187), kind=kCustom, calls=%fused_computation.6 | custom fusion | flops 2097152 | bytes 25166080 | tf_op jit(solution)/shard_map/scatter-add | solution.py:73
  236.0 6.6 %fusion.25 = f32[16,4,128,256]{3,2,1,0:T(8,128)} fusion(bf16[16,128,256,1]{2,1,3,0:T(8,128)(2,1)} %bitcast.209, bf16[16,4,4,128,128]{4,3,2,0,1:T(8,128)(2,1)} %copy_select_fusion), kind=kOutput, calls=%fused_computation.53 | convolution fusion | flops 536870912 | bytes 11534336 | tf_op jit(solution)/shard_map/tsij,tih->tsjh/dot_general | solution.py:70
  242.6 12.5 %scatter_fusion.2 = f32[18,128,256]{2,1,0:T(8,128)S(1)} fusion(f32[18,128,256]{2,1,0:T(8,128)S(1)} %scatter_fusion.1, s32[64]{0:T(128)S(1)} %fusion.34, f32[64,128,256]{2,1,0:T(8,128)} %bitcast.189), kind=kCustom, calls=%fused_computation.7 | custom fusion | flops 2097152 | bytes 25166080 | tf_op jit(solution)/shard_map/scatter-add | solution.py:73
  255.0 6.6 %fusion.27 = f32[16,4,128,256]{3,2,1,0:T(8,128)} fusion(bf16[16,128,256,1]{2,1,3,0:T(8,128)(2,1)} %bitcast.208, bf16[16,4,4,128,128]{4,3,2,0,1:T(8,128)(2,1)} %copy_select_fusion), kind=kOutput, calls=%fused_computation.55 | convolution fusion | flops 536870912 | bytes 11534336 | tf_op jit(solution)/shard_map/tsij,tih->tsjh/dot_general | solution.py:70
  261.6 12.5 %scatter_fusion.3 = f32[18,128,256]{2,1,0:T(8,128)S(1)} fusion(f32[18,128,256]{2,1,0:T(8,128)S(1)} %scatter_fusion.2, s32[64]{0:T(128)S(1)} %fusion.35, f32[64,128,256]{2,1,0:T(8,128)} %bitcast.188), kind=kCustom, calls=%fused_computation.8 | custom fusion | flops 2097152 | bytes 25166080 | tf_op jit(solution)/shard_map/scatter-add | solution.py:73
  274.1 1.6 slice.109
  276.3 4.0 %all-to-all-start.1 = ((bf16[32,8,256]{2,1,0:T(8,128)(2,1)}), bf16[32,8,256]{2,1,0:T(8,128)(2,1)S(1)}, u32[]{:S(2)}, u32[]{:S(2)}) async-start(bf16[32,8,256]{2,1,0:T(8,128)(2,1)} %bitcast.62), calls=%async_computation.1 | async-start | bytes 262144 | tf_op jit(solution)/shard_map/all_to_all | solution.py:77
  280.3 60.4 %all-reduce.6.cloned.1.call-done = (f32[4,64,64]{2,1,0:T(8,128)}, f32[1280,256]{1,0:T(8,128)}, f32[256,4,64]{0,2,1:T(8,128)}, f32[256,4,64]{0,2,1:T(8,128)}, f32[256,256]{0,1:T(8,128)}) async-done(((f32[4,64,64]{2,1,0:T(8,128)}, f32[1280,256]{1,0:T(8,128)}, f32[256,4,64]{0,2,1:T(8,128)}, f32[256,4,64]{0,2,1:T(8,128)}, f32[256,256]{0,1:T(8,128)}), (f32[4,64,64]{2,1,0:T(8,128)}, f32[1280,256]{1,0:T(8,128)}, ...) | async-done | bytes 2162704 | tf_op jit(solution)/shard_map/psum | solution.py:109
  340.7 2.5 fusion.10
  344.2 2.5 fusion.6
  346.8 2.7 scatter_custom_fusion.4
  349.6 1.1 convert_element_type.73
  351.5 1.1 copy.52
  (99 shorter events, 9.1 us)
Async XLA Ops:
  7.2 175.1 %copy-start = (bf16[1280,256]{1,0:T(8,128)(2,1)S(1)}, bf16[1280,256]{1,0:T(8,128)(2,1)}, u32[]{:S(2)}) copy-start(bf16[1280,256]{1,0:T(8,128)(2,1)} %param.14) | copy-start | bytes 1966084
  7.2 132.3 %all-reduce.4.cloned.1.call-start = ((), (), s32[]{:S(2)}) async-start(), calls=%async_computation.2 | async-start | bytes 262144 | tf_op jit(solution)/shard_map/psum | solution.py:48
  9.6 2.0 copy-start.3
  11.6 1.0 copy-start.6
  11.6 1.3 copy-start.8
  11.6 2.4 copy-start.24
  11.6 2.6 copy-start.2
  16.0 134.0 %all-to-all-start = ((bf16[32,8,256]{2,1,0:T(8,128)(2,1)}), bf16[32,8,256]{2,1,0:T(8,128)(2,1)S(1)}, u32[]{:S(2)}, u32[]{:S(2)}) async-start(bf16[32,8,256]{2,1,0:T(8,128)(2,1)} %bitcast.2), calls=%async_computation | async-start | bytes 262144 | tf_op jit(solution)/shard_map/all_to_all | solution.py:25
  23.3 317.3 %all-reduce.6.cloned.1.call-start = ((), (), s32[]{:S(2)}) async-start(), calls=%async_computation.3 | async-start | bytes 4456448 | tf_op jit(solution)/shard_map/psum | solution.py:109
  24.6 4.8 %copy-start.23 = (s32[16,4,4]{0,2,1:T(4,128)S(1)}, s32[16,4,4]{0,2,1:T(4,128)}, u32[]{:S(2)}) copy-start(s32[16,4,4]{0,2,1:T(4,128)} %param.11) | copy-start | bytes 3076
  24.6 5.2 %copy-start.25 = (s32[16,4]{0,1:T(4,128)S(1)}, s32[16,4]{0,1:T(4,128)}, u32[]{:S(2)}) copy-start(s32[16,4]{0,1:T(4,128)} %param.12) | copy-start | bytes 772
  32.5 7.3 %copy-start.5 = (bf16[2048,256]{0,1:T(8,128)(2,1)S(1)}, bf16[2048,256]{0,1:T(8,128)(2,1)}, u32[]{:S(2)}) copy-start(bf16[2048,256]{0,1:T(8,128)(2,1)} %get-tuple-element.21) | copy-start | bytes 3145732
  143.1 3.0 copy-start.17
  155.8 4.0 %copy-start.4 = (bf16[64,128,256]{2,1,0:T(8,128)(2,1)S(1)}, bf16[64,128,256]{2,1,0:T(8,128)(2,1)}, u32[]{:S(2)}) copy-start(bf16[64,128,256]{2,1,0:T(8,128)(2,1)} %gather_fusion.2) | copy-start | bytes 12582916
  177.3 1.6 copy-start.10
  177.3 2.8 copy-start.11
  180.1 2.2 copy-start.13
  182.3 5.6 %copy-start.9 = (bf16[2048,256]{1,0:T(8,128)(2,1)S(1)}, bf16[2048,256]{1,0:T(8,128)(2,1)}, u32[]{:S(2)}) copy-start(bf16[2048,256]{1,0:T(8,128)(2,1)} %param.9) | copy-start | bytes 3145732
  182.3 5.6 %copy-start.22 = (bf16[2048,1280]{1,0:T(8,128)(2,1)S(1)}, bf16[2048,1280]{1,0:T(8,128)(2,1)}, u32[]{:S(2)}) copy-start(bf16[2048,1280]{1,0:T(8,128)(2,1)} %constant_dynamic-update-slice_fusion) | copy-start | bytes 15728644
  276.3 66.9 %copy-start.7 = (bf16[2048,256]{0,1:T(8,128)(2,1)S(1)}, bf16[2048,256]{0,1:T(8,128)(2,1)}, u32[]{:S(2)}) copy-start(bf16[2048,256]{0,1:T(8,128)(2,1)} %copy-done.6) | copy-start | bytes 3145732
  276.3 70.5 %all-to-all-start.1 = ((bf16[32,8,256]{2,1,0:T(8,128)(2,1)}), bf16[32,8,256]{2,1,0:T(8,128)(2,1)S(1)}, u32[]{:S(2)}, u32[]{:S(2)}) async-start(bf16[32,8,256]{2,1,0:T(8,128)(2,1)} %bitcast.62), calls=%async_computation.1 | async-start | bytes 262144 | tf_op jit(solution)/shard_map/all_to_all | solution.py:77
  340.7 2.5 copy-start.12
  340.7 3.5 copy-start.14
  340.7 3.5 copy-start.16
  340.7 3.5 copy-start.18
  349.5 1.1 copy-start.20
  349.6 1.5 copy-start.19
  349.6 1.9 copy-start.21
  350.7 2.0 copy-start.15
  351.5 2.3 copy-start.1
Sparse Core Ops, SparseCore 0:
  14.1 125.2 all-reduce.3
  204.7 135.9 all-reduce.5
where the time goes:
time: 362 us; the launch traced here: 361 us
  waiting for transfers between devices  159 us (44%)
  matrix products  78 us (22%)
  other arithmetic  62.4 us (17%)
  local copies, waits for them, and re-layouts  35.4 us (10%)
  between operations  14.5 us (4%)
  starting transfers between devices  11.4 us (3%)
    psum x1, waiting for transfers between devices, local(): kv_state = lax.psum(local_state, ('row', 'col'))  98.4 us
    psum x1, waiting for transfers between devices, local(): lax.psum((partial_state, stack_part, query_part, key_moment, value_moment...  60.4 us
    scatter-add x4, other arithmetic, local(): ext_grad.at[tile_src[:, relation].reshape(-1)]  49.9 us
    dot_general x4, matrix products, local(): jnp.einsum('tsij,tih->tsjh', masked[:, relation], pulled, preferred_eleme...  25.6 us
    dot_general x4, matrix products, local(): jnp.einsum('tsij,tsjh->tih', masked[:, relation], picked, preferred_eleme...  15.5 us
    gather x4, local copies, waits for them, and re-layouts, local(): picked = extended[tile_src[:, relation]]  11.4 us
    unnamed x60, local copies, waits for them, and re-layouts  10.8 us
    select_n x1, other arithmetic, local(): jnp.where(active[..., None, None], tile_values, jnp.zeros((), tile_values...  7.32 us
  transfers between devices with their start and end apart: 4, of which 2 were waited for; matrix products, arithmetic and copies ran while one was open for 30% of the time, Pallas kernels for 0%

commit v1 on v0

v1 whole, which is shorter than its diff:
```python
import functools

import jax
import jax.numpy as jnp
from jax import lax
from jax.experimental import pallas as pl
from jax.experimental.pallas import tpu as pltpu
from jax.sharding import PartitionSpec as P

HEADS = 4
RELS = 4
TILE = 128
MESH = pl.DeviceIdType.MESH
BF16 = jnp.bfloat16
F32 = jnp.float32
VMEM_LIMIT = 48 * 1024 * 1024
STEP_TILES = 2


def dot(a, b, dims=((1,), (0,)), precision=None):
    return lax.dot_general(a, b, (dims, ((), ())), preferred_element_type=F32, precision=precision)


def pack_rows(rows, bound):
    count, width = rows.shape
    left = rows[:, : width // 2].reshape(count // bound, bound, width // 2)
    right = rows[:, width // 2 :].reshape(count // bound, bound, width // 2)
    return jnp.concatenate([left, right], axis=1)


def unpack_rows(packed, bound):
    count, _, half = packed.shape
    left = packed[:, :bound].reshape(count * bound, half)
    right = packed[:, bound:].reshape(count * bound, half)
    return jnp.concatenate([left, right], axis=1)


class Place:
    def __init__(self, rows, cols):
        self.rows, self.cols, self.planes = rows, cols, cols // 2
        self.devices = rows * cols
        self.row, self.col = lax.axis_index("row"), lax.axis_index("col")
        self.me = self.row * cols + self.col
        self.core = lax.rem(self.col, 2)
        self.plane = lax.div(self.col, 2)

    def peer(self, offset):
        other = lax.rem(self.me + offset, self.devices)
        return (lax.div(other, self.cols), lax.rem(other, self.cols))

    def greet(self):
        barrier = pltpu.get_barrier_semaphore()

        def signal(offset, carry):
            pl.semaphore_signal(barrier, inc=1, device_id=self.peer(offset), device_id_type=MESH)
            return carry

        lax.fori_loop(1, self.devices, signal, 0)

    def met(self):
        pl.semaphore_wait(pltpu.get_barrier_semaphore(), self.devices - 1)


def exchange_copy(place, offset, out, into, sends, recvs):
    other = lax.rem(place.me + offset, place.devices)
    return pltpu.make_async_remote_copy(
        src_ref=out.at[other],
        dst_ref=into.at[place.me],
        send_sem=sends.at[offset],
        recv_sem=recvs.at[offset],
        device_id=place.peer(offset),
        device_id_type=MESH,
    )


def exchange_start(place, out, into, sends, recvs):
    into[place.me] = out[place.me]

    def start(offset, carry):
        exchange_copy(place, offset, out, into, sends, recvs).start()
        return carry

    lax.fori_loop(1, place.devices, start, 0)


def exchange_wait(place, out, into, sends, recvs):
    def wait(offset, carry):
        exchange_copy(place, offset, out, into, sends, recvs).wait()
        return carry

    lax.fori_loop(1, place.devices, wait, 0)


def sum_scratch(rows, width, row_count, col_count):
    half, chunk, planes = rows // 2, rows // col_count, col_count // 2
    count = 1 + 2 * (planes - 1) + (row_count - 1) + planes
    return [
        pltpu.VMEM((half, width), BF16),
        pltpu.VMEM((half, width), BF16),
        pltpu.VMEM((half, width), BF16),
        pltpu.VMEM((planes, chunk, width), BF16),
        pltpu.VMEM((row_count, chunk, width), BF16),
        pltpu.SemaphoreType.DMA((count,)),
        pltpu.SemaphoreType.DMA((count,)),
    ]


def sum_all(place, part, out, scratch):
    out0, in0, out1, in1, in2, sends, recvs = scratch
    rows = part.shape[0]
    half, chunk = rows // 2, rows // place.cols
    core, plane, row, planes = place.core, place.plane, place.row, place.planes
    partner = (row, place.col + 1 - 2 * core)
    used = [0]

    def copy(src, dst, device):
        index = used[0]
        used[0] += 1
        return pltpu.make_async_remote_copy(
            src_ref=src, dst_ref=dst, send_sem=sends.at[index], recv_sem=recvs.at[index],
            device_id=device, device_id_type=MESH,
        )

    out0[...] = part[pl.ds(pl.multiple_of((1 - core) * half, 16), half), :].astype(BF16)
    first = copy(out0, in0, partner)
    first.start()
    first.wait()
    mine = part[pl.ds(pl.multiple_of(core * half, 16), half), :]
    out1[...] = (mine + in0[...].astype(F32)).astype(BF16)

    def piece(index):
        return pl.ds(pl.multiple_of(index * chunk, 16), chunk)

    copies = []
    for step in range(1, planes):
        other = lax.rem(plane + step, planes)
        moved = copy(out1.at[piece(other), :], in1.at[step], (row, other * 2 + core))
        moved.start()
        copies.append(moved)
    total = out1[piece(plane), :].astype(F32)
    for step in range(1, planes):
        copies[step - 1].wait()
        total = total + in1[step].astype(F32)

    in2[row] = total.astype(BF16)
    copies = []
    for step in range(1, place.rows):
        other = lax.rem(row + step, place.rows)
        moved = copy(in2.at[row], in2.at[row], (other, place.col))
        moved.start()
        copies.append(moved)
    for moved in copies:
        moved.wait()
    total = in2[0].astype(F32)
    for step in range(1, place.rows):
        total = total + in2[step].astype(F32)

    def spot(index):
        return pl.ds(pl.multiple_of(core * half + index * chunk, 16), chunk)

    out[spot(plane), :] = total.astype(BF16)
    copies, passed = [], []
    for step in range(1, planes):
        other = lax.rem(plane + step, planes)
        moved = copy(out.at[spot(plane), :], out.at[spot(plane), :], (row, other * 2 + core))
        moved.start()
        copies.append(moved)
    moved = copy(out.at[spot(plane), :], out.at[spot(plane), :], partner)
    moved.start()
    passed.append(moved)
    for step in range(1, planes):
        copies[step - 1].wait()
        source = spot(lax.rem(plane - step + planes, planes))
        moved = copy(out.at[source, :], out.at[source, :], partner)
        moved.start()
        passed.append(moved)
    for moved in passed:
        moved.wait()


def gather_kernel(shape, f_ref, c_ref, rows_ref, halo_ref, moments_ref, outgoing, incoming, sends, recvs, part, *scratch):
    row_count, col_count, bound = shape
    place = Place(row_count, col_count)
    place.greet()
    nodes, width = f_ref.shape
    block = 512
    wanted = rows_ref[...]
    picked = jnp.zeros((wanted.shape[0], width), F32)
    for at in range(0, nodes, block):
        spots = lax.broadcasted_iota(jnp.int32, (wanted.shape[0], block), 1) + at
        picked += dot(jnp.where(spots == wanted, 1.0, 0.0).astype(BF16), f_ref[at : at + block, :])
    outgoing[...] = pack_rows(picked, bound).astype(BF16)
    place.met()
    exchange_start(place, outgoing, incoming, sends, recvs)
    gram = jnp.zeros((width, width), F32)
    cross = jnp.zeros((width, width), F32)
    for at in range(0, nodes, block):
        f = f_ref[at : at + block, :]
        gram += dot(f, f, ((0,), (0,)))
        cross += dot(f, c_ref[at : at + block, :], ((0,), (0,)))
    part[:width, :] = gram
    part[width:, :] = cross
    sum_all(place, part, moments_ref, scratch)
    exchange_wait(place, outgoing, incoming, sends, recvs)
    halo_ref[...] = unpack_rows(incoming[...].astype(F32), bound).astype(BF16)


def layer_kernel(
    scales, bound, index_ref, f_ref, c_ref, halo_ref, moments_ref, w_ref, wqkv_ref, tv_ref,
    out_ref, stack_ref, local_ref, back_ref, qkv_ref, ext, ext_grad, joined, mix, sym,
):
    node_scale, head_scale = scales
    step = pl.program_id(0)
    nodes, width = f_ref.shape
    tiles = nodes // TILE
    span = ext.shape[0] - 1
    head = width // HEADS
    highest = lax.Precision.HIGHEST

    @pl.when(step == 0)
    def _():
        for t in range(tiles):
            ext[t] = f_ref[t * TILE : (t + 1) * TILE, :]
        for t in range(tiles, span):
            ext[t] = halo_ref[(t - tiles) * TILE : (t - tiles + 1) * TILE, :]
        ext[span] = jnp.zeros((TILE, width), BF16)
        ext_grad[...] = jnp.zeros_like(ext_grad)
        stack_ref[...] = jnp.zeros_like(stack_ref)
        gram = moments_ref[:width, :].astype(F32)
        cross = moments_ref[width:, :].astype(F32)
        w_q = wqkv_ref[:, :width].astype(F32)
        w_k = wqkv_ref[:, width : 2 * width].astype(F32)
        w_v = wqkv_ref[:, 2 * width :].astype(F32)
        same = lax.div(lax.broadcasted_iota(jnp.int32, (width, width), 0), head) == lax.div(
            lax.broadcasted_iota(jnp.int32, (width, width), 1), head
        )
        gram_v = dot(gram, w_v, precision=highest)
        gram_k = dot(gram, w_k, precision=highest)
        state = jnp.where(same, dot(w_k, gram_v, ((0,), (0,)), highest), 0.0) * node_scale
        state_grad = jnp.where(same, dot(w_q, cross, ((0,), (0,)), highest), 0.0) * head_scale
        mix[...] = (dot(w_q, state, precision=highest) * head_scale).astype(BF16)
        turned = dot(dot(w_k, state_grad, precision=highest), w_v, ((1,), (1,)), highest)
        sym[...] = ((turned + turned.T) * node_scale).astype(BF16)
        qkv_ref[:, :width] = dot(cross, state, ((1,), (1,)), highest) * head_scale
        qkv_ref[:, width : 2 * width] = dot(gram_v, state_grad, ((1,), (1,)), highest) * node_scale
        qkv_ref[:, 2 * width :] = dot(gram_k, state_grad, precision=highest) * node_scale

    rows = STEP_TILES * TILE
    here = pl.ds(pl.multiple_of(step * rows, rows), rows)
    feats, cots = f_ref[here, :], c_ref[here, :]
    joined[:, :width] = feats

    def slot(tile, relation, s):
        return index_ref[((step * STEP_TILES + tile) * RELS + relation) * 4 + s]

    def adjacency(tile, relation):
        return jnp.concatenate([tv_ref[tile, relation, s] for s in range(4)], axis=1)

    for tile in range(STEP_TILES):
        for relation in range(RELS):
            source = jnp.concatenate([ext[slot(tile, relation, s)] for s in range(4)], axis=0)
            message = dot(adjacency(tile, relation), source)
            joined[tile * TILE : (tile + 1) * TILE, (relation + 1) * width : (relation + 2) * width] = message.astype(BF16)
    pre = dot(joined[...], w_ref[...])
    root = 0.7978845608028654
    square = pre * pre
    bent = jnp.tanh(root * pre * (1.0 + 0.044715 * square))
    upper = 0.5 * (1.0 + bent)
    slope = upper + 0.5 * pre * (1.0 - bent * bent) * root * (1.0 + 3 * 0.044715 * square)
    grad_pre = (cots.astype(F32) * slope).astype(BF16)
    out_ref[...] = (pre * upper + dot(feats, mix[...])).astype(BF16)
    stack_ref[...] += dot(joined[...], grad_pre, ((0,), (0,)))
    own = (
        dot(w_ref[:width, :], grad_pre, ((1,), (1,)))
        + dot(mix[...], cots, ((1,), (1,)))
        + dot(sym[...], feats, ((1,), (1,)))
    )
    for tile in range(STEP_TILES):
        ext_grad[step * STEP_TILES + tile] += own[:, tile * TILE : (tile + 1) * TILE]
    for relation in range(RELS):
        pulled = dot(w_ref[(relation + 1) * width : (relation + 2) * width, :], grad_pre, ((1,), (1,))).astype(BF16)
        for tile in range(STEP_TILES):
            spread = dot(pulled[:, tile * TILE : (tile + 1) * TILE], adjacency(tile, relation))
            for s in range(4):
                ext_grad[slot(tile, relation, s)] += spread[:, s * TILE : (s + 1) * TILE]

    @pl.when(step == pl.num_programs(0) - 1)
    def _():
        for t in range(tiles):
            local_ref[t * TILE : (t + 1) * TILE, :] = ext_grad[t].T
        group = TILE // bound
        for t in range(tiles, span):
            back_ref[(t - tiles) * group : (t - tiles + 1) * group] = pack_rows(ext_grad[t].T, bound).astype(BF16)


def return_kernel(shape, stack_in, back_in, local_in, rows_ref, stack_ref, grad_ref, incoming, sends, recvs, total, *scratch):
    row_count, col_count, bound = shape
    place = Place(row_count, col_count)
    place.greet()
    place.met()
    exchange_start(place, back_in, incoming, sends, recvs)
    sum_all(place, stack_in, total, scratch)
    stack_ref[...] = total[...].astype(F32)
    exchange_wait(place, back_in, incoming, sends, recvs)
    returned = unpack_rows(incoming[...].astype(F32), bound).astype(BF16)
    nodes = local_in.shape[0]
    wanted = rows_ref[...]
    block = 512
    for at in range(0, nodes, block):
        spots = lax.broadcasted_iota(jnp.int32, (block, wanted.shape[1]), 0) + at
        spread = dot(jnp.where(spots == wanted, 1.0, 0.0).astype(BF16), returned)
        grad_ref[at : at + block, :] = (local_in[at : at + block, :] + spread).astype(BF16)


def local(row_count, col_count, features, cotangent, tile_values, tile_src, tile_count, send_rows, w_stack, w_qkv):
    nodes, width = features.shape
    devices = row_count * col_count
    bound = send_rows.shape[2]
    tiles = nodes // TILE
    span = tiles + devices * bound // TILE
    slots = lax.broadcasted_iota(jnp.int32, tile_src.shape, 2)
    index = jnp.where(slots < tile_count[:, :, None], tile_src, span).reshape(-1)
    shape = (row_count, col_count, bound)
    in_vmem = pl.BlockSpec(memory_space=pltpu.VMEM)
    packed = (devices, 2 * bound, width // 2)

    halo, moments = pl.pallas_call(
        functools.partial(gather_kernel, shape),
        out_shape=(
            jax.ShapeDtypeStruct((devices * bound, width), BF16),
            jax.ShapeDtypeStruct((2 * width, width), BF16),
        ),
        in_specs=[in_vmem] * 3,
        out_specs=(in_vmem, in_vmem),
        scratch_shapes=[
            pltpu.VMEM(packed, BF16),
            pltpu.VMEM(packed, BF16),
            pltpu.SemaphoreType.DMA((devices,)),
            pltpu.SemaphoreType.DMA((devices,)),
            pltpu.VMEM((2 * width, width), F32),
            *sum_scratch(2 * width, width, row_count, col_count),
        ],
        compiler_params=pltpu.CompilerParams(
            collective_id=0, has_side_effects=True, vmem_limit_bytes=VMEM_LIMIT
        ),
        name="gather",
    )(features, cotangent, send_rows.reshape(devices * bound, 1))

    rows = STEP_TILES * TILE
    whole = lambda *dims: pl.BlockSpec(dims, lambda i, index: (0,) * len(dims))
    scales = (float(nodes * devices) ** -0.5, float(width // HEADS) ** -0.5)
    stack = w_stack.shape[0]
    layer_out, stack_part, local_grad, back, qkv_grad = pl.pallas_call(
        functools.partial(layer_kernel, scales, bound),
        grid_spec=pltpu.PrefetchScalarGridSpec(
            num_scalar_prefetch=1,
            grid=(tiles // STEP_TILES,),
            in_specs=[
                whole(nodes, width),
                whole(nodes, width),
                whole(devices * bound, width),
                whole(2 * width, width),
                whole(stack, width),
                whole(width, 3 * width),
                pl.BlockSpec((STEP_TILES, RELS, 4, TILE, TILE), lambda i, index: (i, 0, 0, 0, 0)),
            ],
            out_specs=(
                pl.BlockSpec((rows, width), lambda i, index: (i, 0)),
                whole(stack, width),
                whole(nodes, width),
                whole(*packed),
                whole(width, 3 * width),
            ),
            scratch_shapes=[
                pltpu.VMEM((span + 1, TILE, width), BF16),
                pltpu.VMEM((span + 1, width, TILE), F32),
                pltpu.VMEM((rows, stack), BF16),
                pltpu.VMEM((width, width), BF16),
                pltpu.VMEM((width, width), BF16),
            ],
        ),
        out_shape=(
            jax.ShapeDtypeStruct((nodes, width), BF16),
            jax.ShapeDtypeStruct((stack, width), F32),
            jax.ShapeDtypeStruct((nodes, width), F32),
            jax.ShapeDtypeStruct(packed, BF16),
            jax.ShapeDtypeStruct((width, 3 * width), F32),
        ),
        compiler_params=pltpu.CompilerParams(
            dimension_semantics=("arbitrary",), vmem_limit_bytes=VMEM_LIMIT
        ),
        name="layer",
    )(index, features, cotangent, halo, moments, w_stack, w_qkv, tile_values)

    stack_grad, input_grad = pl.pallas_call(
        functools.partial(return_kernel, shape),
        out_shape=(
            jax.ShapeDtypeStruct((stack, width), F32),
            jax.ShapeDtypeStruct((nodes, width), BF16),
        ),
        in_specs=[in_vmem] * 4,
        out_specs=(in_vmem, in_vmem),
        scratch_shapes=[
            pltpu.VMEM(packed, BF16),
            pltpu.SemaphoreType.DMA((devices,)),
            pltpu.SemaphoreType.DMA((devices,)),
            pltpu.VMEM((stack, width), BF16),
            *sum_scratch(stack, width, row_count, col_count),
        ],
        compiler_params=pltpu.CompilerParams(
            collective_id=1, has_side_effects=True, vmem_limit_bytes=VMEM_LIMIT
        ),
        name="giveback",
    )(stack_part, back, local_grad, send_rows.reshape(1, devices * bound))
    return layer_out, input_grad, stack_grad, qkv_grad


def solution(mesh):
    both = ("row", "col")
    placed = (
        P(both, None),
        P(both, None),
        P(both, None, None, None, None),
        P(both, None, None),
        P(both, None),
        P(both, None, None),
        P(),
        P(),
    )
    return jax.shard_map(
        functools.partial(local, mesh.shape["row"], mesh.shape["col"]),
        mesh=mesh,
        in_specs=placed,
        out_specs=(P(both, None), P(both, None), P(), P()),
        check_vma=False,
    )
```

time: 362 us -> 85.5 us (0.24)
  waiting for transfers between devices: 159 us -> 0 us
  matrix products: 78 us -> 0 us
  Pallas kernels: 0 us -> 76.6 us
  other arithmetic: 62.4 us -> 0.7 us
  local copies, waits for them, and re-layouts: 35.4 us -> 7.24 us
  between operations: 14.5 us -> 0.69 us
  starting transfers between devices: 11.4 us -> 0 us
    psum x2 -> x0, waiting for transfers between devices: 159 us -> none  [the longest x1 98.4 us: local(): kv_state = lax.psum(local_state, ('row', 'col'))]
    dot_general x24 -> x0, matrix products: 78 us -> none  [the longest x4 25.6 us: local(): jnp.einsum('tsij,tih->tsjh', masked[:, relation], pulled, preferred_eleme...]
    pallas_call x0 -> x3, Pallas kernels: none -> 76.6 us  [the longest x1 27.6 us: local(): pl.pallas_call(functools.partial(layer_kernel, scales, bound), grid_spec=...]
    scatter-add x5 -> x0, other arithmetic: 52.7 us -> none  [the longest x4 49.9 us: local(): ext_grad.at[tile_src[:, relation].reshape(-1)]]
    gather x5 -> x0, local copies, waits for them, and re-layouts: 13.2 us -> none  [the longest x4 11.4 us: local(): picked = extended[tile_src[:, relation]]]
    all_to_all x2 -> x0, starting transfers between devices: 11.3 us -> none  [the longest x1 7.3 us: local(): lax.all_to_all(outgoing, ('row', 'col'), split_axis=0, concat_axis=0, til...]
    select_n x8 -> x1, other arithmetic: 7.35 us -> 0.7 us  [local(): jnp.where(slots < tile_count[:, :, None], tile_src, span).reshape(-1)]
    slice x9 -> x0, local copies, waits for them, and re-layouts: 5.79 us -> none  [the longest x1 1.65 us: local(): query = qkv[:, :width].reshape(node_dev, HEADS, head_dim)]
  transfers between devices with their start and end apart: 4 -> 0, of which waited for: 2 -> 0; matrix products, arithmetic and copies ran while one was open for 30% -> 0% of each run, Pallas kernels for 0% -> 0%
where the time goes in v1:
time: 85.5 us; the launch traced here: 85.2 us
  Pallas kernels  76.6 us (90%)
  local copies, waits for them, and re-layouts  7.24 us (8%)
    pallas_call x1, Pallas kernels, local(): pl.pallas_call(functools.partial(layer_kernel, scales, bound), grid_spec=...  27.6 us
    pallas_call x1, Pallas kernels, local(): pl.pallas_call(functools.partial(return_kernel, shape), out_shape=(jax.Sh...  26.4 us
    pallas_call x1, Pallas kernels, local(): pl.pallas_call(functools.partial(gather_kernel, shape), out_shape=(jax.Sh...  22.6 us
    unnamed x13, local copies, waits for them, and re-layouts  6.83 us

profile of v1, /device:TPU:0, one launch (start us, length us, event | category | flops | bytes accessed | tf_op | source)
XLA Modules:
  0.0 85.2 jit_solution(2956296385857118492)
XLA Ops:
  0.6 0.7 fusion
  1.3 0.8 copy.15
  2.1 0.1 reshape.20.rows_ref
  2.2 0.1 copy.14
  2.3 0.1 reshape.18.index_ref
  2.4 0.1 reshape.21.rows_ref
  2.5 0.0 copy-start
  2.5 1.2 %copy-done = bf16[2048,256]{1,0:T(8,128)(2,1)S(1)} copy-done((bf16[2048,256]{1,0:T(8,128)(2,1)S(1)}, bf16[2048,256]{1,0:T(8,128)(2,1)}, u32[]{:S(2)}) %copy-start) | copy-done | bytes 1048600
  3.7 0.0 copy-start.1
  3.7 1.2 %copy-done.1 = bf16[2048,256]{1,0:T(8,128)(2,1)S(1)} copy-done((bf16[2048,256]{1,0:T(8,128)(2,1)S(1)}, bf16[2048,256]{1,0:T(8,128)(2,1)}, u32[]{:S(2)}) %copy-start.1) | copy-done | bytes 1048600
  5.0 0.0 copy-start.3
  5.0 0.0 copy-start.4
  5.0 22.6 %gather.1 = (bf16[256,256]{1,0:T(8,128)(2,1)S(1)}, bf16[512,256]{1,0:T(8,128)(2,1)S(1)}) custom-call(bf16[2048,256]{1,0:T(8,128)(2,1)S(1)} %copy-done, bf16[2048,256]{1,0:T(8,128)(2,1)S(1)} %copy-done.1, s32[256,1]{1,0:T(8,128)S(1)} %reshape.21.rows_ref), custom_call_target="tpu_custom_call" | custom-call | tf_op jit(solution)/shard_map/gather/pallas_call | solution.py:327
  27.6 0.0 copy-done.3
  27.6 0.0 copy-done.4
  27.6 27.6 %layer.1 = (bf16[2048,256]{1,0:T(8,128)(2,1)}, f32[1280,256]{1,0:T(8,128)S(1)}, f32[2048,256]{1,0:T(8,128)}, bf16[32,16,128]{2,1,0:T(8,128)(2,1)S(1)}, f32[256,768]{1,0:T(8,128)}) custom-call(s32[256]{0:T(256)S(1)} %reshape.18.index_ref, bf16[2048,256]{1,0:T(8,128)(2,1)S(1)} %copy-done, bf16[2048,256]{1,0:T(8,128)(2,1)S(1)} %copy-done.1, ...), custom_call_target="tpu_custom_call" | custom-call | tf_op jit(solution)/shard_map/layer/pallas_call | solution.py:353
  55.2 0.0 copy-start.2
  55.2 1.6 %copy-done.2 = f32[2048,256]{1,0:T(8,128)S(1)} copy-done((f32[2048,256]{1,0:T(8,128)S(1)}, f32[2048,256]{1,0:T(8,128)}, u32[]{:S(2)}) %copy-start.2) | copy-done | bytes 2097176
  56.8 26.4 %giveback.1 = (f32[1280,256]{1,0:T(8,128)S(1)}, bf16[2048,256]{1,0:T(8,128)(2,1)S(1)}) custom-call(f32[1280,256]{1,0:T(8,128)S(1)} %get-tuple-element.16.stack_in, bf16[32,16,128]{2,1,0:T(8,128)(2,1)S(1)} %get-tuple-element.17.back_in, f32[2048,256]{1,0:T(8,128)S(1)} %copy-done.2, s32[1,256]{1,0:T(1,128)S(1)} %reshape.20.rows_ref), custom_call_target="tpu_custom_call" | custom-call | tf_op jit(solution)/shard_map/giveback/pallas_call | solution.py:395
  83.2 1.0 %copy.20 = bf16[2048,256]{1,0:T(8,128)(2,1)} copy(bf16[2048,256]{1,0:T(8,128)(2,1)S(1)} %get-tuple-element.27) | data formatting | bytes 2097152
  84.2 1.1 %copy.21 = f32[1280,256]{1,0:T(8,128)} copy(f32[1280,256]{1,0:T(8,128)S(1)} %get-tuple-element.28) | data formatting | bytes 2621440
Async XLA Ops:
  2.5 1.2 %copy-start = (bf16[2048,256]{1,0:T(8,128)(2,1)S(1)}, bf16[2048,256]{1,0:T(8,128)(2,1)}, u32[]{:S(2)}) copy-start(bf16[2048,256]{1,0:T(8,128)(2,1)} %f_ref.3) | copy-start | bytes 3145732
  3.7 1.2 %copy-start.1 = (bf16[2048,256]{1,0:T(8,128)(2,1)S(1)}, bf16[2048,256]{1,0:T(8,128)(2,1)}, u32[]{:S(2)}) copy-start(bf16[2048,256]{1,0:T(8,128)(2,1)} %c_ref.3) | copy-start | bytes 3145732
  5.0 22.6 %copy-start.3 = (bf16[1280,256]{1,0:T(8,128)(2,1)S(1)}, bf16[1280,256]{1,0:T(8,128)(2,1)}, u32[]{:S(2)}) copy-start(bf16[1280,256]{1,0:T(8,128)(2,1)} %w_ref.1) | copy-start | bytes 1966084
  5.0 22.6 %copy-start.4 = (bf16[256,768]{1,0:T(8,128)(2,1)S(1)}, bf16[256,768]{1,0:T(8,128)(2,1)}, u32[]{:S(2)}) copy-start(bf16[256,768]{1,0:T(8,128)(2,1)} %wqkv_ref.1) | copy-start | bytes 1179652
  55.2 1.6 %copy-start.2 = (f32[2048,256]{1,0:T(8,128)S(1)}, f32[2048,256]{1,0:T(8,128)}, u32[]{:S(2)}) copy-start(f32[2048,256]{1,0:T(8,128)} %get-tuple-element.18.local_in) | copy-start | bytes 6291460

commit v2 on v1

v2 whole, which is shorter than its diff:
```python
import functools

import jax
import jax.numpy as jnp
from jax import lax
from jax.experimental import pallas as pl
from jax.experimental.pallas import tpu as pltpu
from jax.sharding import PartitionSpec as P

HEADS = 4
RELS = 4
TILE = 128
MESH = pl.DeviceIdType.MESH
BF16 = jnp.bfloat16
F32 = jnp.float32
VMEM_LIMIT = 48 * 1024 * 1024
STEP_TILES = 2


def dot(a, b, dims=((1,), (0,)), precision=None):
    return lax.dot_general(a, b, (dims, ((), ())), preferred_element_type=F32, precision=precision)


def pack_rows(rows, bound):
    count, width = rows.shape
    left = rows[:, : width // 2].reshape(count // bound, bound, width // 2)
    right = rows[:, width // 2 :].reshape(count // bound, bound, width // 2)
    return jnp.concatenate([left, right], axis=1)


def unpack_rows(packed, bound):
    count, _, half = packed.shape
    left = packed[:, :bound].reshape(count * bound, half)
    right = packed[:, bound:].reshape(count * bound, half)
    return jnp.concatenate([left, right], axis=1)


class Place:
    def __init__(self, rows, cols):
        self.rows, self.cols, self.planes = rows, cols, cols // 2
        self.devices = rows * cols
        self.row, self.col = lax.axis_index("row"), lax.axis_index("col")
        self.me = self.row * cols + self.col
        self.core = lax.rem(self.col, 2)
        self.plane = lax.div(self.col, 2)

    def peer(self, offset):
        other = lax.rem(self.me + offset, self.devices)
        return (lax.div(other, self.cols), lax.rem(other, self.cols))

    def greet(self):
        barrier = pltpu.get_barrier_semaphore()

        def signal(offset, carry):
            pl.semaphore_signal(barrier, inc=1, device_id=self.peer(offset), device_id_type=MESH)
            return carry

        lax.fori_loop(1, self.devices, signal, 0)

    def met(self):
        pl.semaphore_wait(pltpu.get_barrier_semaphore(), self.devices - 1)


def exchange_copy(place, offset, out, into, sends, recvs):
    other = lax.rem(place.me + offset, place.devices)
    return pltpu.make_async_remote_copy(
        src_ref=out.at[other],
        dst_ref=into.at[place.me],
        send_sem=sends.at[offset],
        recv_sem=recvs.at[offset],
        device_id=place.peer(offset),
        device_id_type=MESH,
    )


def exchange_start(place, out, into, sends, recvs):
    into[place.me] = out[place.me]

    def start(offset, carry):
        exchange_copy(place, offset, out, into, sends, recvs).start()
        return carry

    lax.fori_loop(1, place.devices, start, 0)


def exchange_wait(place, out, into, sends, recvs):
    def wait(offset, carry):
        exchange_copy(place, offset, out, into, sends, recvs).wait()
        return carry

    lax.fori_loop(1, place.devices, wait, 0)


def row_share(rows, row_count, col_count, kind):
    chunk = rows // col_count
    align = 16 if kind == BF16 else 8
    return chunk // row_count if chunk % (row_count * align) == 0 else 0


def sum_scratch(rows, width, row_count, col_count, kind):
    half, chunk, planes = rows // 2, rows // col_count, col_count // 2
    share = row_share(rows, row_count, col_count, kind)
    count = 1 + 2 * (planes - 1) + 2 * (row_count - 1) + planes
    return [
        pltpu.VMEM((half, width), kind),
        pltpu.VMEM((half, width), kind),
        pltpu.VMEM((half, width), kind),
        pltpu.VMEM((planes, chunk, width), kind),
        pltpu.VMEM((chunk, width), kind),
        pltpu.VMEM((row_count, share or chunk, width), kind),
        pltpu.SemaphoreType.DMA((count,)),
        pltpu.SemaphoreType.DMA((count,)),
    ]


def sum_all(place, part, out, scratch):
    out0, in0, out1, in1, out2, in2, sends, recvs = scratch
    kind = out.dtype
    rows = part.shape[0]
    half, chunk = rows // 2, rows // place.cols
    share = row_share(rows, place.rows, place.cols, kind)
    core, plane, row, planes = place.core, place.plane, place.row, place.planes
    partner = (row, place.col + 1 - 2 * core)
    used = [0]

    def copy(src, dst, device):
        index = used[0]
        used[0] += 1
        moved = pltpu.make_async_remote_copy(
            src_ref=src, dst_ref=dst, send_sem=sends.at[index], recv_sem=recvs.at[index],
            device_id=device, device_id_type=MESH,
        )
        moved.start()
        return moved

    out0[...] = part[pl.ds(pl.multiple_of((1 - core) * half, 16), half), :].astype(kind)
    first = copy(out0, in0, partner)
    yield
    first.wait()
    mine = part[pl.ds(pl.multiple_of(core * half, 16), half), :]
    out1[...] = (mine + in0[...].astype(F32)).astype(kind)

    def piece(index, size=chunk):
        return pl.ds(pl.multiple_of(index * size, 8), size)

    copies = []
    for step in range(1, planes):
        other = lax.rem(plane + step, planes)
        copies.append(copy(out1.at[piece(other), :], in1.at[step], (row, other * 2 + core)))
    yield
    total = out1[piece(plane), :].astype(F32)
    for step in range(1, planes):
        copies[step - 1].wait()
        total = total + in1[step].astype(F32)

    def spot(index):
        return pl.ds(pl.multiple_of(core * half + index * chunk, 8), chunk)

    out2[...] = total.astype(kind)
    others = [lax.rem(row + step, place.rows) for step in range(1, place.rows)]
    if share:
        copies = [
            copy(out2.at[piece(other, share), :], in2.at[step], (other, place.col))
            for step, other in enumerate(others)
        ]
        yield
        total = out2[piece(row, share), :].astype(F32)
        for step, moved in enumerate(copies):
            moved.wait()
            total = total + in2[step].astype(F32)
        part_spot = pl.ds(pl.multiple_of(core * half + plane * chunk + row * share, 8), share)
        out[part_spot, :] = total.astype(kind)
        copies = [copy(out.at[part_spot, :], out.at[part_spot, :], (other, place.col)) for other in others]
        yield
        for moved in copies:
            moved.wait()
    else:
        in2[row] = out2[...]
        copies = [copy(out2, in2.at[row], (other, place.col)) for other in others]
        yield
        for moved in copies:
            moved.wait()
        total = in2[0].astype(F32)
        for step in range(1, place.rows):
            total = total + in2[step].astype(F32)
        out[spot(plane), :] = total.astype(kind)

    mine = out.at[spot(plane), :]
    copies = []
    for step in range(1, planes):
        other = lax.rem(plane + step, planes)
        copies.append(copy(mine, mine, (row, other * 2 + core)))
    passed = [copy(mine, mine, partner)]
    yield
    for step in range(1, planes):
        copies[step - 1].wait()
        source = spot(lax.rem(plane - step + planes, planes))
        passed.append(copy(out.at[source, :], out.at[source, :], partner))
    yield
    for moved in passed:
        moved.wait()


def gather_kernel(shape, f_ref, c_ref, rows_ref, halo_ref, moments_ref, outgoing, incoming, sends, recvs):
    row_count, col_count, bound = shape
    place = Place(row_count, col_count)
    place.greet()
    nodes, width = f_ref.shape
    block = 512
    wanted = rows_ref[...]
    picked = jnp.zeros((wanted.shape[0], width), F32)
    for at in range(0, nodes, block):
        spots = lax.broadcasted_iota(jnp.int32, (wanted.shape[0], block), 1) + at
        picked += dot(jnp.where(spots == wanted, 1.0, 0.0).astype(BF16), f_ref[at : at + block, :])
    outgoing[...] = pack_rows(picked, bound).astype(BF16)
    place.met()
    exchange_start(place, outgoing, incoming, sends, recvs)
    gram = jnp.zeros((width, width), F32)
    cross = jnp.zeros((width, width), F32)
    for at in range(0, nodes, block):
        f = f_ref[at : at + block, :]
        gram += dot(f, f, ((0,), (0,)))
        cross += dot(f, c_ref[at : at + block, :], ((0,), (0,)))
    moments_ref[:width, :] = gram
    moments_ref[width:, :] = cross
    exchange_wait(place, outgoing, incoming, sends, recvs)
    halo_ref[...] = unpack_rows(incoming[...].astype(F32), bound).astype(BF16)


def layer_kernel(
    bound, index_ref, f_ref, c_ref, halo_ref, w_ref, tv_ref,
    act_ref, stack_ref, local_ref, back_ref, ext, ext_grad, joined,
):
    step = pl.program_id(0)
    nodes, width = f_ref.shape
    tiles = nodes // TILE
    span = ext.shape[0] - 1

    @pl.when(step == 0)
    def _():
        for t in range(tiles):
            ext[t] = f_ref[t * TILE : (t + 1) * TILE, :]
        for t in range(tiles, span):
            ext[t] = halo_ref[(t - tiles) * TILE : (t - tiles + 1) * TILE, :]
        ext[span] = jnp.zeros((TILE, width), BF16)
        ext_grad[...] = jnp.zeros_like(ext_grad)
        stack_ref[...] = jnp.zeros_like(stack_ref)

    rows = STEP_TILES * TILE
    here = pl.ds(pl.multiple_of(step * rows, rows), rows)
    feats, cots = f_ref[here, :], c_ref[here, :]
    joined[:, :width] = feats

    def slot(tile, relation, s):
        return index_ref[((step * STEP_TILES + tile) * RELS + relation) * 4 + s]

    def adjacency(tile, relation):
        return jnp.concatenate([tv_ref[tile, relation, s] for s in range(4)], axis=1)

    for tile in range(STEP_TILES):
        for relation in range(RELS):
            source = jnp.concatenate([ext[slot(tile, relation, s)] for s in range(4)], axis=0)
            message = dot(adjacency(tile, relation), source)
            joined[tile * TILE : (tile + 1) * TILE, (relation + 1) * width : (relation + 2) * width] = message.astype(BF16)
    pre = dot(joined[...], w_ref[...])
    root = 0.7978845608028654
    square = pre * pre
    bent = jnp.tanh(root * pre * (1.0 + 0.044715 * square))
    upper = 0.5 * (1.0 + bent)
    slope = upper + 0.5 * pre * (1.0 - bent * bent) * root * (1.0 + 3 * 0.044715 * square)
    grad_pre = (cots.astype(F32) * slope).astype(BF16)
    act_ref[...] = pre * upper
    stack = w_ref.shape[0]
    weight = dot(joined[...], grad_pre, ((0,), (0,)))
    stack_ref[:stack, :] += weight[:, : width // 2]
    stack_ref[stack:, :] += weight[:, width // 2 :]
    own = dot(w_ref[:width, :], grad_pre, ((1,), (1,)))
    for tile in range(STEP_TILES):
        ext_grad[step * STEP_TILES + tile] += own[:, tile * TILE : (tile + 1) * TILE]
    for relation in range(RELS):
        pulled = dot(w_ref[(relation + 1) * width : (relation + 2) * width, :], grad_pre, ((1,), (1,))).astype(BF16)
        for tile in range(STEP_TILES):
            spread = dot(pulled[:, tile * TILE : (tile + 1) * TILE], adjacency(tile, relation))
            for s in range(4):
                ext_grad[slot(tile, relation, s)] += spread[:, s * TILE : (s + 1) * TILE]

    @pl.when(step == pl.num_programs(0) - 1)
    def _():
        for t in range(tiles):
            local_ref[t * TILE : (t + 1) * TILE, :] = ext_grad[t].T
        group = TILE // bound
        for t in range(tiles, span):
            back_ref[(t - tiles) * group : (t - tiles + 1) * group] = pack_rows(ext_grad[t].T, bound).astype(BF16)


def split(value):
    high = value.astype(BF16)
    return high, (value - high.astype(F32)).astype(BF16)


def dot_wide(a, b, dims=((1,), (0,))):
    if a.dtype == BF16:
        b_high, b_low = split(b)
        return dot(a, b_high, dims) + dot(a, b_low, dims)
    if b.dtype == BF16:
        a_high, a_low = split(a)
        return dot(a_high, b, dims) + dot(a_low, b, dims)
    a_high, a_low = split(a)
    b_high, b_low = split(b)
    return dot(a_high, b_high, dims) + (dot(a_high, b_low, dims) + dot(a_low, b_high, dims))


def finish(scales, moments, wqkv, feats, cots, act, held, loads, landed, rows_ref, out_ref, grad_ref, qkv_ref):
    node_scale, head_scale = scales
    nodes, width = feats.shape
    head = width // HEADS
    gram, cross = moments[:width, :], moments[width:, :]
    w_q, w_k, w_v = (wqkv[:, at * width : (at + 1) * width] for at in range(3))
    same = lax.div(lax.broadcasted_iota(jnp.int32, (width, width), 0), head) == lax.div(
        lax.broadcasted_iota(jnp.int32, (width, width), 1), head
    )
    gram_v, gram_k = dot_wide(gram, w_v), dot_wide(gram, w_k)
    state = jnp.where(same, dot_wide(w_k, gram_v, ((0,), (0,))), 0.0) * node_scale
    state_grad = jnp.where(same, dot_wide(w_q, cross, ((0,), (0,))), 0.0) * head_scale
    yield
    mix = (dot_wide(w_q, state) * head_scale).astype(BF16)
    turned = dot_wide(dot_wide(w_k, state_grad), w_v, ((1,), (1,)))
    sym = ((turned + turned.T) * node_scale).astype(BF16)
    yield
    qkv_ref[:, :width] = dot_wide(cross, state, ((1,), (1,))) * head_scale
    qkv_ref[:, width : 2 * width] = dot_wide(gram_v, state_grad, ((1,), (1,))) * node_scale
    qkv_ref[:, 2 * width :] = dot_wide(gram_k, state_grad) * node_scale
    for load in loads:
        load.wait()
    returned = landed()
    yield
    wanted = rows_ref[...]
    block = 512
    for at in range(0, nodes, block):
        here = slice(at, at + block)
        spots = lax.broadcasted_iota(jnp.int32, (block, wanted.shape[1]), 0) + at
        spread = dot(jnp.where(spots == wanted, 1.0, 0.0).astype(BF16), returned)
        out_ref[here, :] = (act[here, :] + dot(feats[here, :], mix)).astype(BF16)
        attention = dot(cots[here, :], mix, ((1,), (1,))) + dot(feats[here, :], sym)
        grad_ref[here, :] = (held[here, :] + spread + attention).astype(BF16)
        yield


def return_kernel(
    shape, scales, streams, moments_in, stack_in, back_in, rows_ref, wqkv, f_in, c_in, act_in, local_in,
    stack_ref, grad_ref, out_ref, qkv_ref,
    incoming, sends, recvs, load_sems, feats, cots, act, held, total, moments, *scratch,
):
    row_count, col_count, bound = shape
    place = Place(row_count, col_count)
    place.greet()
    loads = []
    for at, (src, dst) in enumerate(((f_in, feats), (c_in, cots), (act_in, act), (local_in, held))):
        loads.append(pltpu.make_async_copy(src, dst, load_sems.at[at]))
        loads[-1].start()
    place.met()
    exchange_start(place, back_in, incoming, sends, recvs)

    def landed():
        exchange_wait(place, back_in, incoming, sends, recvs)
        return unpack_rows(incoming[...].astype(F32), bound).astype(BF16)

    early = sum_all(place, moments_in, moments, scratch[:streams])
    late = sum_all(place, stack_in, total, scratch[streams:])
    done = object()
    next(early)
    while next(early, done) is not done:
        next(late, done)
    work = finish(scales, moments, wqkv, feats, cots, act, held, loads, landed, rows_ref, out_ref, grad_ref, qkv_ref)
    active = [work, late]
    while active:
        active = [steps for steps in active if next(steps, done) is not done]
    stack = stack_ref.shape[0]
    stack_ref[...] = jnp.concatenate([total[:stack, :], total[stack:, :]], axis=1)


def local(row_count, col_count, features, cotangent, tile_values, tile_src, tile_count, send_rows, w_stack, w_qkv):
    nodes, width = features.shape
    devices = row_count * col_count
    bound = send_rows.shape[2]
    tiles = nodes // TILE
    span = tiles + devices * bound // TILE
    slots = lax.broadcasted_iota(jnp.int32, tile_src.shape, 2)
    index = jnp.where(slots < tile_count[:, :, None], tile_src, span).reshape(-1)
    shape = (row_count, col_count, bound)
    in_vmem = pl.BlockSpec(memory_space=pltpu.VMEM)
    packed = (devices, 2 * bound, width // 2)

    stack = w_stack.shape[0]
    scales = (float(nodes * devices) ** -0.5, float(width // HEADS) ** -0.5)
    halo, moments = pl.pallas_call(
        functools.partial(gather_kernel, shape),
        out_shape=(
            jax.ShapeDtypeStruct((devices * bound, width), BF16),
            jax.ShapeDtypeStruct((2 * width, width), F32),
        ),
        in_specs=[in_vmem] * 3,
        out_specs=(in_vmem, in_vmem),
        scratch_shapes=[
            pltpu.VMEM(packed, BF16),
            pltpu.VMEM(packed, BF16),
            pltpu.SemaphoreType.DMA((devices,)),
            pltpu.SemaphoreType.DMA((devices,)),
        ],
        compiler_params=pltpu.CompilerParams(
            collective_id=0, has_side_effects=True, vmem_limit_bytes=VMEM_LIMIT
        ),
        name="gather",
    )(features, cotangent, send_rows.reshape(devices * bound, 1))

    rows = STEP_TILES * TILE
    whole = lambda *dims: pl.BlockSpec(dims, lambda i, index: (0,) * len(dims))
    by_rows = pl.BlockSpec((rows, width), lambda i, index: (i, 0))
    act, stack_part, local_grad, back = pl.pallas_call(
        functools.partial(layer_kernel, bound),
        grid_spec=pltpu.PrefetchScalarGridSpec(
            num_scalar_prefetch=1,
            grid=(tiles // STEP_TILES,),
            in_specs=[
                whole(nodes, width),
                whole(nodes, width),
                whole(devices * bound, width),
                whole(stack, width),
                pl.BlockSpec((STEP_TILES, RELS, 4, TILE, TILE), lambda i, index: (i, 0, 0, 0, 0)),
            ],
            out_specs=(
                by_rows,
                whole(2 * stack, width // 2),
                whole(nodes, width),
                whole(*packed),
            ),
            scratch_shapes=[
                pltpu.VMEM((span + 1, TILE, width), BF16),
                pltpu.VMEM((span + 1, width, TILE), F32),
                pltpu.VMEM((rows, stack), BF16),
            ],
        ),
        out_shape=(
            jax.ShapeDtypeStruct((nodes, width), F32),
            jax.ShapeDtypeStruct((2 * stack, width // 2), F32),
            jax.ShapeDtypeStruct((nodes, width), F32),
            jax.ShapeDtypeStruct(packed, BF16),
        ),
        compiler_params=pltpu.CompilerParams(
            dimension_semantics=("arbitrary",), vmem_limit_bytes=VMEM_LIMIT
        ),
        name="layer",
    )(index, features, cotangent, halo, w_stack, tile_values)

    moment_scratch = sum_scratch(2 * width, width, row_count, col_count, F32)
    stack_scratch = sum_scratch(2 * stack, width // 2, row_count, col_count, BF16)
    in_any = pl.BlockSpec(memory_space=pl.ANY)
    stack_grad, input_grad, layer_out, qkv_grad = pl.pallas_call(
        functools.partial(return_kernel, shape, scales, len(moment_scratch)),
        out_shape=(
            jax.ShapeDtypeStruct((stack, width), BF16),
            jax.ShapeDtypeStruct((nodes, width), BF16),
            jax.ShapeDtypeStruct((nodes, width), BF16),
            jax.ShapeDtypeStruct((width, 3 * width), F32),
        ),
        in_specs=[in_vmem] * 5 + [in_any] * 4,
        out_specs=(in_vmem,) * 4,
        scratch_shapes=[
            pltpu.VMEM(packed, BF16),
            pltpu.SemaphoreType.DMA((devices,)),
            pltpu.SemaphoreType.DMA((devices,)),
            pltpu.SemaphoreType.DMA((4,)),
            pltpu.VMEM((nodes, width), BF16),
            pltpu.VMEM((nodes, width), BF16),
            pltpu.VMEM((nodes, width), F32),
            pltpu.VMEM((nodes, width), F32),
            pltpu.VMEM((2 * stack, width // 2), BF16),
            pltpu.VMEM((2 * width, width), F32),
            *moment_scratch,
            *stack_scratch,
        ],
        compiler_params=pltpu.CompilerParams(
            collective_id=1, has_side_effects=True, vmem_limit_bytes=VMEM_LIMIT
        ),
        name="giveback",
    )(moments, stack_part, back, send_rows.reshape(1, devices * bound), w_qkv, features, cotangent, act, local_grad)
    return layer_out, input_grad, stack_grad.astype(F32), qkv_grad


def solution(mesh):
    both = ("row", "col")
    placed = (
        P(both, None),
        P(both, None),
        P(both, None, None, None, None),
        P(both, None, None),
        P(both, None),
        P(both, None, None),
        P(),
        P(),
    )
    return jax.shard_map(
        functools.partial(local, mesh.shape["row"], mesh.shape["col"]),
        mesh=mesh,
        in_specs=placed,
        out_specs=(P(both, None), P(both, None), P(), P()),
        check_vma=False,
    )
```

time: 85.5 us -> 82.1 us (0.960)
  Pallas kernels: 76.6 us -> 71.8 us
  other arithmetic: 0.7 us -> 1.86 us
    pallas_call x1, Pallas kernels: 22.6 us -> 10.7 us  [local(): pl.pallas_call(functools.partial(gather_kernel, shape), out_shape=(jax.Sh...]
    pallas_call x2, Pallas kernels: 54 us -> 61.1 us  [the longest x1 36.5 us: local(): pl.pallas_call(functools.partial(return_kernel, shape, scales, len(moment...]
    convert_element_type x0 -> x1, other arithmetic: none -> 1.15 us  [local(): return (layer_out, input_grad, stack_grad.astype(F32), qkv_grad)]
    unnamed x13 -> x14, local copies, waits for them, and re-layouts: 6.83 us -> 7.09 us
where the time goes in v2:
time: 82.1 us; the launch traced here: 81.8 us
  Pallas kernels  71.8 us (87%)
  local copies, waits for them, and re-layouts  7.5 us (9%)
  other arithmetic  1.86 us (2%)
    pallas_call x1, Pallas kernels, local(): pl.pallas_call(functools.partial(return_kernel, shape, scales, len(moment...  36.5 us
    pallas_call x1, Pallas kernels, local(): pl.pallas_call(functools.partial(layer_kernel, bound), grid_spec=pltpu.Pr...  24.6 us
    pallas_call x1, Pallas kernels, local(): pl.pallas_call(functools.partial(gather_kernel, shape), out_shape=(jax.Sh...  10.7 us
    unnamed x14, local copies, waits for them, and re-layouts  7.09 us

profile of v2, /device:TPU:0, one launch (start us, length us, event | category | flops | bytes accessed | tf_op | source)
XLA Modules:
  0.0 81.8 jit_solution(11490138288725312936)
XLA Ops:
  0.6 0.7 fusion
  1.3 0.8 copy.14
  2.1 0.1 reshape.20.rows_ref
  2.2 0.1 copy.16
  2.3 0.1 reshape.19.index_ref
  2.4 0.1 reshape.21.rows_ref
  2.5 0.0 copy-start
  2.5 1.2 %copy-done = bf16[2048,256]{1,0:T(8,128)(2,1)S(1)} copy-done((bf16[2048,256]{1,0:T(8,128)(2,1)S(1)}, bf16[2048,256]{1,0:T(8,128)(2,1)}, u32[]{:S(2)}) %copy-start) | copy-done | bytes 1048600
  3.7 0.0 copy-start.1
  3.7 1.2 %copy-done.1 = bf16[2048,256]{1,0:T(8,128)(2,1)S(1)} copy-done((bf16[2048,256]{1,0:T(8,128)(2,1)S(1)}, bf16[2048,256]{1,0:T(8,128)(2,1)}, u32[]{:S(2)}) %copy-start.1) | copy-done | bytes 1048600
  5.0 0.0 copy-start.3
  5.0 10.7 %gather.1 = (bf16[256,256]{1,0:T(8,128)(2,1)S(1)}, f32[512,256]{1,0:T(8,128)S(1)}) custom-call(bf16[2048,256]{1,0:T(8,128)(2,1)S(1)} %copy-done, bf16[2048,256]{1,0:T(8,128)(2,1)S(1)} %copy-done.1, s32[256,1]{1,0:T(8,128)S(1)} %reshape.21.rows_ref), custom_call_target="tpu_custom_call" | custom-call | tf_op jit(solution)/shard_map/gather/pallas_call | solution.py:396
  15.7 0.0 copy-done.3
  15.7 0.0 copy-start.4
  15.7 24.6 %layer.1 = (f32[2048,256]{1,0:T(8,128)}, f32[2560,128]{1,0:T(8,128)S(1)}, f32[2048,256]{1,0:T(8,128)}, bf16[32,16,128]{2,1,0:T(8,128)(2,1)S(1)}) custom-call(s32[256]{0:T(256)S(1)} %reshape.19.index_ref, bf16[2048,256]{1,0:T(8,128)(2,1)S(1)} %copy-done, bf16[2048,256]{1,0:T(8,128)(2,1)S(1)} %copy-done.1, bf16[256,256]{1,0:T(8,128)(2,1)S(1)} %get-tuple-element.15.halo_ref, ...), custom_call_target="tpu_custom_call" | custom-call | tf_op jit(solution)/shard_map/layer/pallas_call | solution.py:419
  40.3 0.0 copy-start.2
  40.3 1.1 %copy-done.2 = f32[2560,128]{1,0:T(8,128)} copy-done((f32[2560,128]{1,0:T(8,128)}, f32[2560,128]{1,0:T(8,128)S(1)}, u32[]{:S(2)}) %copy-start.2) | copy-done | bytes 1310744
  41.3 0.0 copy-done.4
  41.3 36.5 %giveback.1 = (bf16[1280,256]{1,0:T(8,128)(2,1)S(1)}, bf16[2048,256]{1,0:T(8,128)(2,1)S(1)}, bf16[2048,256]{1,0:T(8,128)(2,1)S(1)}, f32[256,768]{1,0:T(8,128)S(1)}) custom-call(f32[512,256]{1,0:T(8,128)S(1)} %get-tuple-element.14.moments_in, f32[2560,128]{1,0:T(8,128)} %copy-done.2, bf16[32,16,128]{2,1,0:T(8,128)(2,1)S(1)} %get-tuple-element.17.back_in, ...), custom_call_target="tpu_custom_call" | custom-call | tf_op jit(solution)/shard_map/giveback/pallas_call | solution.py:458
  77.8 1.2 %convert_element_type.3 = f32[1280,256]{1,0:T(8,128)} convert(bf16[1280,256]{1,0:T(8,128)(2,1)S(1)} %get-tuple-element.22) | non-fusion elementwise | flops 327680 | bytes 1966080 | tf_op jit(solution)/shard_map/convert_element_type | solution.py:487
  79.0 1.0 %copy.21 = bf16[2048,256]{1,0:T(8,128)(2,1)} copy(bf16[2048,256]{1,0:T(8,128)(2,1)S(1)} %get-tuple-element.28) | data formatting | bytes 2097152
  79.9 1.0 %copy.22 = bf16[2048,256]{1,0:T(8,128)(2,1)} copy(bf16[2048,256]{1,0:T(8,128)(2,1)S(1)} %get-tuple-element.29) | data formatting | bytes 2097152
  80.9 0.9 %copy.23 = f32[256,768]{1,0:T(8,128)} copy(f32[256,768]{1,0:T(8,128)S(1)} %get-tuple-element.31) | data formatting | bytes 1572864
Async XLA Ops:
  2.5 1.2 %copy-start = (bf16[2048,256]{1,0:T(8,128)(2,1)S(1)}, bf16[2048,256]{1,0:T(8,128)(2,1)}, u32[]{:S(2)}) copy-start(bf16[2048,256]{1,0:T(8,128)(2,1)} %f_in.1) | copy-start | bytes 3145732
  3.7 1.2 %copy-start.1 = (bf16[2048,256]{1,0:T(8,128)(2,1)S(1)}, bf16[2048,256]{1,0:T(8,128)(2,1)}, u32[]{:S(2)}) copy-start(bf16[2048,256]{1,0:T(8,128)(2,1)} %c_in.1) | copy-start | bytes 3145732
  5.0 10.7 %copy-start.3 = (bf16[1280,256]{1,0:T(8,128)(2,1)S(1)}, bf16[1280,256]{1,0:T(8,128)(2,1)}, u32[]{:S(2)}) copy-start(bf16[1280,256]{1,0:T(8,128)(2,1)} %w_ref.1) | copy-start | bytes 1966084
  15.7 25.6 %copy-start.4 = (bf16[256,768]{1,0:T(8,128)(2,1)S(1)}, bf16[256,768]{1,0:T(8,128)(2,1)}, u32[]{:S(2)}) copy-start(bf16[256,768]{1,0:T(8,128)(2,1)} %wqkv.1) | copy-start | bytes 1179652
  40.3 1.1 %copy-start.2 = (f32[2560,128]{1,0:T(8,128)}, f32[2560,128]{1,0:T(8,128)S(1)}, u32[]{:S(2)}) copy-start(f32[2560,128]{1,0:T(8,128)S(1)} %get-tuple-element.16.stack_in) | copy-start | bytes 3932164

commit v3 on v2

--- a/solution.py
+++ b/solution.py
@@ -14,7 +14,7 @@
 BF16 = jnp.bfloat16
 F32 = jnp.float32
 VMEM_LIMIT = 48 * 1024 * 1024
-STEP_TILES = 2
+STEP_TILES = 4
 
 
 def dot(a, b, dims=((1,), (0,)), precision=None):
@@ -201,13 +201,16 @@
         moved.wait()
 
 
-def gather_kernel(shape, f_ref, c_ref, rows_ref, halo_ref, moments_ref, outgoing, incoming, sends, recvs):
+def gather_kernel(shape, f_ref, c_ref, rows_ref, halo_ref, moments_ref, outgoing, incoming, sends, recvs, cots, load_sem):
     row_count, col_count, bound = shape
     place = Place(row_count, col_count)
     place.greet()
+    load = pltpu.make_async_copy(c_ref, cots, load_sem)
+    load.start()
     nodes, width = f_ref.shape
     block = 512
-    wanted = rows_ref[...]
+    turned = jnp.broadcast_to(rows_ref[...].astype(F32), (TILE, rows_ref.shape[1])).T.astype(jnp.int32)
+    wanted = jnp.concatenate([turned] * (block // TILE), axis=1)
     picked = jnp.zeros((wanted.shape[0], width), F32)
     for at in range(0, nodes, block):
         spots = lax.broadcasted_iota(jnp.int32, (wanted.shape[0], block), 1) + at
@@ -217,10 +220,11 @@
     exchange_start(place, outgoing, incoming, sends, recvs)
     gram = jnp.zeros((width, width), F32)
     cross = jnp.zeros((width, width), F32)
+    load.wait()
     for at in range(0, nodes, block):
         f = f_ref[at : at + block, :]
         gram += dot(f, f, ((0,), (0,)))
-        cross += dot(f, c_ref[at : at + block, :], ((0,), (0,)))
+        cross += dot(f, cots[at : at + block, :], ((0,), (0,)))
     moments_ref[:width, :] = gram
     moments_ref[width:, :] = cross
     exchange_wait(place, outgoing, incoming, sends, recvs)
@@ -229,7 +233,7 @@
 
 def layer_kernel(
     bound, index_ref, f_ref, c_ref, halo_ref, w_ref, tv_ref,
-    act_ref, stack_ref, local_ref, back_ref, ext, ext_grad, joined,
+    act_ref, stack_ref, ext_grad, back_ref, ext, joined,
 ):
     step = pl.program_id(0)
     nodes, width = f_ref.shape
@@ -286,8 +290,6 @@
 
     @pl.when(step == pl.num_programs(0) - 1)
     def _():
-        for t in range(tiles):
-            local_ref[t * TILE : (t + 1) * TILE, :] = ext_grad[t].T
         group = TILE // bound
         for t in range(tiles, span):
             back_ref[(t - tiles) * group : (t - tiles + 1) * group] = pack_rows(ext_grad[t].T, bound).astype(BF16)
@@ -310,7 +312,22 @@
     return dot(a_high, b_high, dims) + (dot(a_high, b_low, dims) + dot(a_low, b_high, dims))
 
 
-def finish(scales, moments, wqkv, feats, cots, act, held, loads, landed, rows_ref, out_ref, grad_ref, qkv_ref):
+def prepare(held, base, loads, landed, rows_ref):
+    for load in loads:
+        load.wait()
+    returned = landed()
+    yield
+    wanted = rows_ref[...]
+    block = 4 * TILE
+    for at in range(0, base.shape[0], block):
+        spots = lax.broadcasted_iota(jnp.int32, (block, wanted.shape[1]), 0) + at
+        spread = dot(jnp.where(spots == wanted, 1.0, 0.0).astype(BF16), returned)
+        own = jnp.concatenate([held[t].T for t in range(at // TILE, (at + block) // TILE)], axis=0)
+        base[at : at + block, :] = own + spread
+        yield
+
+
+def finish(scales, moments, wqkv, feats, cots, act, base, out_ref, grad_ref, qkv_ref):
     node_scale, head_scale = scales
     nodes, width = feats.shape
     head = width // HEADS
@@ -330,32 +347,26 @@
     qkv_ref[:, :width] = dot_wide(cross, state, ((1,), (1,))) * head_scale
     qkv_ref[:, width : 2 * width] = dot_wide(gram_v, state_grad, ((1,), (1,))) * node_scale
     qkv_ref[:, 2 * width :] = dot_wide(gram_k, state_grad) * node_scale
-    for load in loads:
-        load.wait()
-    returned = landed()
-    yield
-    wanted = rows_ref[...]
+    yield
     block = 512
     for at in range(0, nodes, block):
         here = slice(at, at + block)
-        spots = lax.broadcasted_iota(jnp.int32, (block, wanted.shape[1]), 0) + at
-        spread = dot(jnp.where(spots == wanted, 1.0, 0.0).astype(BF16), returned)
         out_ref[here, :] = (act[here, :] + dot(feats[here, :], mix)).astype(BF16)
         attention = dot(cots[here, :], mix, ((1,), (1,))) + dot(feats[here, :], sym)
-        grad_ref[here, :] = (held[here, :] + spread + attention).astype(BF16)
+        grad_ref[here, :] = (base[here, :] + attention).astype(BF16)
         yield
 
 
 def return_kernel(
     shape, scales, streams, moments_in, stack_in, back_in, rows_ref, wqkv, f_in, c_in, act_in, local_in,
     stack_ref, grad_ref, out_ref, qkv_ref,
-    incoming, sends, recvs, load_sems, feats, cots, act, held, total, moments, *scratch,
+    incoming, sends, recvs, load_sems, feats, cots, act, held, base, total, moments, *scratch,
 ):
     row_count, col_count, bound = shape
     place = Place(row_count, col_count)
     place.greet()
     loads = []
-    for at, (src, dst) in enumerate(((f_in, feats), (c_in, cots), (act_in, act), (local_in, held))):
+    for at, (src, dst) in enumerate(((f_in, feats), (c_in, cots), (act_in, act), (local_in.at[pl.ds(0, held.shape[0])], held))):
         loads.append(pltpu.make_async_copy(src, dst, load_sems.at[at]))
         loads[-1].start()
     place.met()
@@ -368,10 +379,15 @@
     early = sum_all(place, moments_in, moments, scratch[:streams])
     late = sum_all(place, stack_in, total, scratch[streams:])
     done = object()
+    ready = prepare(held, base, loads, landed, rows_ref)
     next(early)
+    next(late)
     while next(early, done) is not done:
         next(late, done)
-    work = finish(scales, moments, wqkv, feats, cots, act, held, loads, landed, rows_ref, out_ref, grad_ref, qkv_ref)
+        next(ready, done)
+    for _ in ready:
+        pass
+    work = finish(scales, moments, wqkv, feats, cots, act, base, out_ref, grad_ref, qkv_ref)
     active = [work, late]
     while active:
         active = [steps for steps in active if next(steps, done) is not done]
@@ -389,6 +405,8 @@
     index = jnp.where(slots < tile_count[:, :, None], tile_src, span).reshape(-1)
     shape = (row_count, col_count, bound)
     in_vmem = pl.BlockSpec(memory_space=pltpu.VMEM)
+    in_any = pl.BlockSpec(memory_space=pl.ANY)
+    flat_rows = send_rows.reshape(1, devices * bound)
     packed = (devices, 2 * bound, width // 2)
 
     stack = w_stack.shape[0]
@@ -399,19 +417,21 @@
             jax.ShapeDtypeStruct((devices * bound, width), BF16),
             jax.ShapeDtypeStruct((2 * width, width), F32),
         ),
-        in_specs=[in_vmem] * 3,
+        in_specs=[in_vmem, in_any, in_vmem],
         out_specs=(in_vmem, in_vmem),
         scratch_shapes=[
             pltpu.VMEM(packed, BF16),
             pltpu.VMEM(packed, BF16),
             pltpu.SemaphoreType.DMA((devices,)),
             pltpu.SemaphoreType.DMA((devices,)),
+            pltpu.VMEM((nodes, width), BF16),
+            pltpu.SemaphoreType.DMA,
         ],
         compiler_params=pltpu.CompilerParams(
             collective_id=0, has_side_effects=True, vmem_limit_bytes=VMEM_LIMIT
         ),
         name="gather",
-    )(features, cotangent, send_rows.reshape(devices * bound, 1))
+    )(features, cotangent, flat_rows)
 
     rows = STEP_TILES * TILE
     whole = lambda *dims: pl.BlockSpec(dims, lambda i, index: (0,) * len(dims))
@@ -431,19 +451,18 @@
             out_specs=(
                 by_rows,
                 whole(2 * stack, width // 2),
-                whole(nodes, width),
+                whole(span + 1, width, TILE),
                 whole(*packed),
             ),
             scratch_shapes=[
                 pltpu.VMEM((span + 1, TILE, width), BF16),
-                pltpu.VMEM((span + 1, width, TILE), F32),
                 pltpu.VMEM((rows, stack), BF16),
             ],
         ),
         out_shape=(
             jax.ShapeDtypeStruct((nodes, width), F32),
             jax.ShapeDtypeStruct((2 * stack, width // 2), F32),
-            jax.ShapeDtypeStruct((nodes, width), F32),
+            jax.ShapeDtypeStruct((span + 1, width, TILE), F32),
             jax.ShapeDtypeStruct(packed, BF16),
         ),
         compiler_params=pltpu.CompilerParams(
@@ -454,7 +473,6 @@
 
     moment_scratch = sum_scratch(2 * width, width, row_count, col_count, F32)
     stack_scratch = sum_scratch(2 * stack, width // 2, row_count, col_count, BF16)
-    in_any = pl.BlockSpec(memory_space=pl.ANY)
     stack_grad, input_grad, layer_out, qkv_grad = pl.pallas_call(
         functools.partial(return_kernel, shape, scales, len(moment_scratch)),
         out_shape=(
@@ -473,6 +491,7 @@
             pltpu.VMEM((nodes, width), BF16),
             pltpu.VMEM((nodes, width), BF16),
             pltpu.VMEM((nodes, width), F32),
+            pltpu.VMEM((tiles, width, TILE), F32),
             pltpu.VMEM((nodes, width), F32),
             pltpu.VMEM((2 * stack, width // 2), BF16),
             pltpu.VMEM((2 * width, width), F32),
@@ -483,7 +502,7 @@
             collective_id=1, has_side_effects=True, vmem_limit_bytes=VMEM_LIMIT
         ),
         name="giveback",
-    )(moments, stack_part, back, send_rows.reshape(1, devices * bound), w_qkv, features, cotangent, act, local_grad)
+    )(moments, stack_part, back, flat_rows, w_qkv, features, cotangent, act, local_grad)
     return layer_out, input_grad, stack_grad.astype(F32), qkv_grad
 
 

time: 82.1 us -> 75.8 us (0.923)
  Pallas kernels: 71.8 us -> 65.5 us
    pallas_call x1, Pallas kernels: 24.6 us -> 20.7 us  [local(): pl.pallas_call(functools.partial(layer_kernel, bound), grid_spec=pltpu.Pr...]
    pallas_call x1, Pallas kernels: 36.5 us -> 34.1 us  [local(): pl.pallas_call(functools.partial(return_kernel, shape, scales, len(moment...]
where the time goes in v3:
time: 75.8 us; the launch traced here: 75.5 us
  Pallas kernels  65.5 us (86%)
  local copies, waits for them, and re-layouts  7.4 us (10%)
  other arithmetic  1.86 us (2%)
    pallas_call x1, Pallas kernels, local(): pl.pallas_call(functools.partial(return_kernel, shape, scales, len(moment...  34.1 us
    pallas_call x1, Pallas kernels, local(): pl.pallas_call(functools.partial(layer_kernel, bound), grid_spec=pltpu.Pr...  20.7 us
    pallas_call x1, Pallas kernels, local(): pl.pallas_call(functools.partial(gather_kernel, shape), out_shape=(jax.Sh...  10.7 us
    unnamed x14, local copies, waits for them, and re-layouts  7.09 us

profile of v3, /device:TPU:0, one launch (start us, length us, event | category | flops | bytes accessed | tf_op | source)
XLA Modules:
  0.0 75.5 jit_solution(3563771373432038684)
XLA Ops:
  0.6 0.7 fusion
  1.3 0.8 %copy.13 = s32[1,32,8]{2,1,0:T(8,128)S(1)} copy(s32[1,32,8]{1,2,0:T(8,128)} %param.13) | data formatting | bytes 2048 | tf_op args[5]
  2.1 0.1 reshape.15.rows_ref
  2.2 0.1 copy.14
  2.3 0.1 reshape.16.index_ref
  2.4 0.0 copy-start
  2.4 1.2 %copy-done = bf16[2048,256]{1,0:T(8,128)(2,1)S(1)} copy-done((bf16[2048,256]{1,0:T(8,128)(2,1)S(1)}, bf16[2048,256]{1,0:T(8,128)(2,1)}, u32[]{:S(2)}) %copy-start) | copy-done | bytes 1048600
  3.6 0.0 copy-start.1
  3.6 1.2 %copy-done.1 = bf16[2048,256]{1,0:T(8,128)(2,1)S(1)} copy-done((bf16[2048,256]{1,0:T(8,128)(2,1)S(1)}, bf16[2048,256]{1,0:T(8,128)(2,1)}, u32[]{:S(2)}) %copy-start.1) | copy-done | bytes 1048600
  4.9 0.0 copy-start.3
  4.9 10.7 %gather.1 = (bf16[256,256]{1,0:T(8,128)(2,1)S(1)}, f32[512,256]{1,0:T(8,128)S(1)}) custom-call(bf16[2048,256]{1,0:T(8,128)(2,1)S(1)} %copy-done, bf16[2048,256]{1,0:T(8,128)(2,1)S(1)} %copy-done.1, s32[1,256]{1,0:T(1,128)S(1)} %reshape.15.rows_ref), custom_call_target="tpu_custom_call" | custom-call | tf_op jit(solution)/shard_map/gather/pallas_call | solution.py:414
  15.6 0.0 copy-done.3
  15.6 0.0 copy-start.4
  15.6 20.7 %layer.1 = (f32[2048,256]{1,0:T(8,128)}, f32[2560,128]{1,0:T(8,128)S(1)}, f32[19,256,128]{2,1,0:T(8,128)}, bf16[32,16,128]{2,1,0:T(8,128)(2,1)S(1)}) custom-call(s32[256]{0:T(256)S(1)} %reshape.16.index_ref, bf16[2048,256]{1,0:T(8,128)(2,1)S(1)} %copy-done, bf16[2048,256]{1,0:T(8,128)(2,1)S(1)} %copy-done.1, ...), custom_call_target="tpu_custom_call" | custom-call | tf_op jit(solution)/shard_map/layer/pallas_call | solution.py:439
  36.3 0.0 copy-start.2
  36.3 1.1 %copy-done.2 = f32[2560,128]{1,0:T(8,128)} copy-done((f32[2560,128]{1,0:T(8,128)}, f32[2560,128]{1,0:T(8,128)S(1)}, u32[]{:S(2)}) %copy-start.2) | copy-done | bytes 1310744
  37.4 0.0 copy-done.4
  37.4 34.1 %giveback.1 = (bf16[1280,256]{1,0:T(8,128)(2,1)S(1)}, bf16[2048,256]{1,0:T(8,128)(2,1)S(1)}, bf16[2048,256]{1,0:T(8,128)(2,1)S(1)}, f32[256,768]{1,0:T(8,128)S(1)}) custom-call(f32[512,256]{1,0:T(8,128)S(1)} %get-tuple-element.14.moments_in, f32[2560,128]{1,0:T(8,128)} %copy-done.2, bf16[32,16,128]{2,1,0:T(8,128)(2,1)S(1)} %get-tuple-element.17.back_in, ...), custom_call_target="tpu_custom_call" | custom-call | tf_op jit(solution)/shard_map/giveback/pallas_call | solution.py:476
  71.5 1.2 %convert_element_type.3 = f32[1280,256]{1,0:T(8,128)} convert(bf16[1280,256]{1,0:T(8,128)(2,1)S(1)} %get-tuple-element.22) | non-fusion elementwise | flops 327680 | bytes 1966080 | tf_op jit(solution)/shard_map/convert_element_type | solution.py:506
  72.6 1.0 %copy.18 = bf16[2048,256]{1,0:T(8,128)(2,1)} copy(bf16[2048,256]{1,0:T(8,128)(2,1)S(1)} %get-tuple-element.28) | data formatting | bytes 2097152
  73.6 1.0 %copy.19 = bf16[2048,256]{1,0:T(8,128)(2,1)} copy(bf16[2048,256]{1,0:T(8,128)(2,1)S(1)} %get-tuple-element.29) | data formatting | bytes 2097152
  74.6 0.9 %copy.20 = f32[256,768]{1,0:T(8,128)} copy(f32[256,768]{1,0:T(8,128)S(1)} %get-tuple-element.31) | data formatting | bytes 1572864
Async XLA Ops:
  2.4 1.2 %copy-start = (bf16[2048,256]{1,0:T(8,128)(2,1)S(1)}, bf16[2048,256]{1,0:T(8,128)(2,1)}, u32[]{:S(2)}) copy-start(bf16[2048,256]{1,0:T(8,128)(2,1)} %f_in.1) | copy-start | bytes 3145732
  3.6 1.2 %copy-start.1 = (bf16[2048,256]{1,0:T(8,128)(2,1)S(1)}, bf16[2048,256]{1,0:T(8,128)(2,1)}, u32[]{:S(2)}) copy-start(bf16[2048,256]{1,0:T(8,128)(2,1)} %c_in.1) | copy-start | bytes 3145732
  4.9 10.7 %copy-start.3 = (bf16[1280,256]{1,0:T(8,128)(2,1)S(1)}, bf16[1280,256]{1,0:T(8,128)(2,1)}, u32[]{:S(2)}) copy-start(bf16[1280,256]{1,0:T(8,128)(2,1)} %w_ref.1) | copy-start | bytes 1966084
  15.6 21.8 %copy-start.4 = (bf16[256,768]{1,0:T(8,128)(2,1)S(1)}, bf16[256,768]{1,0:T(8,128)(2,1)}, u32[]{:S(2)}) copy-start(bf16[256,768]{1,0:T(8,128)(2,1)} %wqkv.1) | copy-start | bytes 1179652
  36.3 1.1 %copy-start.2 = (f32[2560,128]{1,0:T(8,128)}, f32[2560,128]{1,0:T(8,128)S(1)}, u32[]{:S(2)}) copy-start(f32[2560,128]{1,0:T(8,128)S(1)} %get-tuple-element.16.stack_in) | copy-start | bytes 3932164
